TPU v7x, 32 devices: a whole 2x2x4 slice. The times are simulated.
32 devices in a mesh: section: 4 (over y, core), dp: 8 (over z, x).
Axes of the slice: x: 2, y: 2, z: 4, core: 2. Of those that a mesh axis runs over, the one named last changes fastest.
Arguments:
- horizon: bfloat16 [4, 8192, 256], P('section', 'dp'), may hold values from -6 to 6
- cotangent: bfloat16 [4, 8192, 256], P('section', 'dp'), may hold values from -6 to 6
- obs_tokens: bfloat16 [4, 256, 2, 256], P('section', 'dp'), may hold values from -6 to 6
- obs_repeat: int32 [4, 8, 32], P(None, 'dp'), may hold values from 1 to 4, 64 in all within a row
- noise_step: int32 [4, 512], P(None, 'dp'), may hold values from 0 to 99
- time_weight: bfloat16 [256, 256], replicated, may hold values from -0.375 to 0.375
- self_in: bfloat16 [4, 256, 768], P('section'), may hold values from -0.375 to 0.375
- self_out: bfloat16 [4, 256, 256], P('section'), may hold values from -0.75 to 0.75
- cross_q: bfloat16 [4, 256, 256], P('section'), may hold values from -0.375 to 0.375
- cross_kv: bfloat16 [4, 256, 512], P('section'), may hold values from -0.375 to 0.375
- cross_out: bfloat16 [4, 256, 256], P('section'), may hold values from -0.5 to 0.5
- mlp_up: bfloat16 [4, 256, 1024], P('section'), may hold values from -0.375 to 0.375
- mlp_down: bfloat16 [4, 1024, 256], P('section'), may hold values from -0.1875 to 0.1875
- gains: float32 [4, 3, 256], P('section'), may hold values from 0.5 to 1.5
- shifts: float32 [4, 10, 256], P('section'), may hold values from -2 to 2
- mlp_bias: float32 [4, 1024], P('section'), may hold values from -2 to 2
Outputs:
- predictions: bfloat16 [4, 8192, 256], P('section', 'dp')
- horizon_grad: bfloat16 [4, 8192, 256], P('section', 'dp')
- self_in_grad: float32 [4, 256, 768], P('section', 'dp')
- self_out_grad: float32 [4, 256, 256], P('section', 'dp')
- cross_q_grad: float32 [4, 256, 256], P('section', 'dp')
- cross_kv_grad: float32 [4, 256, 512], P('section', 'dp')
- cross_out_grad: float32 [4, 256, 256], P('section', 'dp')
- mlp_up_grad: float32 [4, 256, 1024], P('section', 'dp')
- mlp_down_grad: float32 [4, 1024, 256], P('section', 'dp')
- gains_grad: float32 [4, 3, 256], P('section', None, 'dp')
- shifts_grad: float32 [4, 10, 256], P('section', None, 'dp')
- mlp_bias_grad: float32 [4, 1024], P('section', 'dp')
- time_weight_grad: float32 [256, 256], P('dp')
Inputs may be any that keep to these rules, and one draw needn't show every extreme that they name: `obs_repeat`: each row of 32 counts sums to 64.
All inputs are finite; a program needn't handle non-finite values.
Results may differ from a plain program's by a relative error of at most 0.025.
Values may be sent and summed in bfloat16 or wider, within the bound.
A program may use at most 384 MiB of HBM per device.

v0:
```python
from functools import partial
import math

import jax
import jax.numpy as jnp
from jax import lax
from jax.sharding import PartitionSpec as P

HEADS = 4


def passed_along(block, axis, distance):
    devices = range(lax.axis_size(axis))
    route = [(i - distance, i) for i in devices if i - distance in devices]
    return lax.ppermute(block, axis, route)


def layer_norm(values, gain_row, shift_row):
    center = values - jnp.mean(values, axis=-1, keepdims=True)
    spread = jnp.mean(center * center, axis=-1, keepdims=True)
    return center * lax.rsqrt(spread + 1e-05) * gain_row + shift_row


def product(left_side, right_side):
    return jnp.dot(left_side, right_side, preferred_element_type=jnp.float32)


def exact_product(left_side, right_side):
    return jnp.dot(
        left_side, right_side, precision=lax.Precision.HIGHEST, preferred_element_type=jnp.float32
    )


def contract_rows(left_side, right_side):
    return lax.dot_general(
        left_side, right_side, (((0,), (0,)), ((), ())), preferred_element_type=jnp.float32
    )


def contract_cols(left_side, right_side):
    return lax.dot_general(
        left_side, right_side, (((1,), (1,)), ((), ())), preferred_element_type=jnp.float32
    )


def sinus_table(noise_steps, columns):
    half_cols = columns // 2
    frequency = jnp.exp(-math.log(10000.0) * jnp.arange(half_cols).astype(jnp.float32) / half_cols)
    angles = noise_steps.astype(jnp.float32)[:, None] * frequency[None, :]
    return jnp.concatenate([jnp.sin(angles), jnp.cos(angles)], axis=1)


def build_context(micro_index, noise_step, obs_repeat, obs_all, time_weight, columns):
    noise_steps = lax.dynamic_index_in_dim(noise_step, micro_index, 0, keepdims=False)
    counts = lax.dynamic_index_in_dim(obs_repeat, micro_index, 0, keepdims=False)[0]
    observed = lax.dynamic_index_in_dim(obs_all, micro_index, 0, keepdims=False)
    observed = observed.reshape(-1, columns)
    sinus_low = sinus_table(noise_steps, columns).astype(jnp.bfloat16)
    memory = product(sinus_low, time_weight).astype(jnp.bfloat16)
    samples = noise_steps.shape[0]
    running_ends = jnp.cumsum(counts)
    owner_index = jnp.sum(
        (jnp.arange(samples)[:, None] >= running_ends[None, :]).astype(jnp.int32), axis=1
    )
    select = (owner_index[:, None] == jnp.arange(counts.shape[0])[None, :]).astype(jnp.float32)
    return (sinus_low, memory, select, observed)


def head_tables(columns, horizon_len):
    head_dim = columns // HEADS
    head_select = (jnp.arange(columns)[:, None] // head_dim == jnp.arange(HEADS)[None, :]).astype(
        jnp.float32
    )
    wide = HEADS * horizon_len
    block_ones = (
        jnp.arange(wide)[:, None] // horizon_len == jnp.arange(wide)[None, :] // horizon_len
    ).astype(jnp.float32)
    causal_wide = jnp.arange(horizon_len)[:, None] >= (jnp.arange(wide) % horizon_len)[None, :]
    return (head_select, block_ones, causal_wide)


def spread_heads(values3, head_select):
    head_mask = jnp.transpose(head_select).astype(values3.dtype)
    samples, horizon_len, columns = values3.shape
    return (values3[:, None, :, :] * head_mask[None, :, None, :]).reshape(
        samples, HEADS * horizon_len, columns
    )


def fold_heads(wide3, head_select):
    samples, wide, columns = wide3.shape
    head_mask = jnp.transpose(head_select)
    return jnp.sum(
        wide3.reshape(samples, HEADS, wide // HEADS, columns) * head_mask[None, :, None, :], axis=1
    )


def head_sums(values3, head_select):
    samples, horizon_len, columns = values3.shape
    return exact_product(values3.reshape(-1, columns), head_select).reshape(
        samples, horizon_len, HEADS
    )


def head_expand(values3, head_select):
    samples, horizon_len, heads = values3.shape
    return exact_product(values3.reshape(-1, heads), jnp.transpose(head_select)).reshape(
        samples, horizon_len, -1
    )


def self_scores(queries3, keys_wide, causal_wide, score_scale):
    scores = (
        jnp.einsum("sqd,sjd->sqj", queries3, keys_wide, preferred_element_type=jnp.float32)
        * score_scale
    )
    return jnp.where(causal_wide[None], scores, -1e30)


def cross_scores(query3, joined_keys, head_select, score_scale):
    query_f = query3.astype(jnp.float32)
    return [
        head_sums(query_f * joined_keys[:, index, None, :].astype(jnp.float32), head_select)
        * score_scale
        for index in range(joined_keys.shape[1])
    ]


def layer_forward(residual, layer_index, weights, context):
    w_in, w_so, w_cq, w_ckv, w_co, w_up, w_dn, gain_all, shift_all, bias_up = weights
    sinus_low, memory, select, observed = context
    gain_rows = gain_all[layer_index]
    shift_rows = shift_all[layer_index]
    samples = memory.shape[0]
    tokens, columns = residual.shape
    horizon_len = tokens // samples
    head_dim = columns // HEADS
    score_scale = head_dim ** (-0.5)
    head_select, block_ones, causal_wide = head_tables(columns, horizon_len)
    obs_count = select.shape[1]
    obs_width = observed.shape[0] // obs_count
    normed = layer_norm(residual, gain_rows[0], shift_rows[0]).astype(jnp.bfloat16)
    qkv_all = product(normed, w_in[layer_index])
    queries = (qkv_all[:, :columns] + shift_rows[3]).astype(jnp.bfloat16)
    keys_self = qkv_all[:, columns : 2 * columns].astype(jnp.bfloat16)
    vals_self = (qkv_all[:, 2 * columns :] + shift_rows[4]).astype(jnp.bfloat16)
    keys_wide = spread_heads(keys_self.reshape(samples, horizon_len, columns), head_select)
    vals_wide = spread_heads(vals_self.reshape(samples, horizon_len, columns), head_select)
    scores = self_scores(
        queries.reshape(samples, horizon_len, columns), keys_wide, causal_wide, score_scale
    )
    row_top = jnp.max(scores, axis=-1, keepdims=True)
    totals = exact_product(
        jnp.exp(scores - row_top).reshape(-1, block_ones.shape[0]), block_ones
    ).reshape(scores.shape)
    log_self = row_top + jnp.log(totals)
    probs_low = jnp.exp(scores - log_self).astype(jnp.bfloat16)
    context_self = (
        jnp.einsum("sqj,sjd->sqd", probs_low, vals_wide, preferred_element_type=jnp.float32)
        .reshape(tokens, columns)
        .astype(jnp.bfloat16)
    )
    after_self = residual + (product(context_self, w_so[layer_index]) + shift_rows[5])
    cross_in = layer_norm(after_self, gain_rows[1], shift_rows[1]).astype(jnp.bfloat16)
    cross_query = (product(cross_in, w_cq[layer_index]) + shift_rows[6]).astype(jnp.bfloat16)
    time_kv = product(memory, w_ckv[layer_index])
    obs_kv = product(observed, w_ckv[layer_index])
    time_keys = time_kv[:, :columns].astype(jnp.bfloat16)
    time_vals = (time_kv[:, columns:] + shift_rows[7]).astype(jnp.bfloat16)
    obs_keys = obs_kv[:, :columns].astype(jnp.bfloat16).reshape(obs_count, obs_width * columns)
    obs_vals = (
        (obs_kv[:, columns:] + shift_rows[7])
        .astype(jnp.bfloat16)
        .reshape(obs_count, obs_width * columns)
    )
    select_low = select.astype(jnp.bfloat16)
    sample_keys = (
        product(select_low, obs_keys).astype(jnp.bfloat16).reshape(samples, obs_width, columns)
    )
    sample_vals = (
        product(select_low, obs_vals).astype(jnp.bfloat16).reshape(samples, obs_width, columns)
    )
    joined_keys = jnp.concatenate([time_keys[:, None, :], sample_keys], axis=1)
    joined_vals = jnp.concatenate([time_vals[:, None, :], sample_vals], axis=1)
    score_list = cross_scores(
        cross_query.reshape(samples, horizon_len, columns), joined_keys, head_select, score_scale
    )
    cross_top = score_list[0]
    for entry in score_list[1:]:
        cross_top = jnp.maximum(cross_top, entry)
    cross_total = sum((jnp.exp(entry - cross_top) for entry in score_list))
    log_cross = cross_top + jnp.log(cross_total)
    mixed = jnp.zeros((samples, horizon_len, columns), jnp.float32)
    for index, entry in enumerate(score_list):
        weight_low = jnp.exp(entry - log_cross).astype(jnp.bfloat16).astype(jnp.float32)
        mixed = mixed + head_expand(weight_low, head_select) * joined_vals[
            :, index, None, :
        ].astype(jnp.float32)
    context_cross = mixed.reshape(tokens, columns).astype(jnp.bfloat16)
    after_cross = after_self + (product(context_cross, w_co[layer_index]) + shift_rows[8])
    mlp_in = layer_norm(after_cross, gain_rows[2], shift_rows[2]).astype(jnp.bfloat16)
    hidden_pre = product(mlp_in, w_up[layer_index]) + bias_up[layer_index]
    hidden = jax.nn.gelu(hidden_pre).astype(jnp.bfloat16)
    output = after_cross + (product(hidden, w_dn[layer_index]) + shift_rows[9])
    kept_values = (
        residual,
        queries,
        keys_self,
        vals_self,
        log_self,
        context_self,
        after_self,
        cross_query,
        joined_keys,
        joined_vals,
        log_cross,
        context_cross,
        after_cross,
        hidden_pre,
    )
    return (output, kept_values)


def layer_backward(grad_out, layer_index, weights, context, kept_values):
    w_in, w_so, w_cq, w_ckv, w_co, w_up, w_dn, gain_all, shift_all, bias_up = weights
    sinus_low, memory, select, observed = context
    (
        residual,
        queries,
        keys_self,
        vals_self,
        log_self,
        context_self,
        after_self,
        cross_query,
        joined_keys,
        joined_vals,
        log_cross,
        context_cross,
        after_cross,
        hidden_pre,
    ) = kept_values
    gain_rows = gain_all[layer_index]
    shift_rows = shift_all[layer_index]
    samples = memory.shape[0]
    tokens, columns = residual.shape
    horizon_len = tokens // samples
    head_dim = columns // HEADS
    score_scale = head_dim ** (-0.5)
    head_select, block_ones, causal_wide = head_tables(columns, horizon_len)
    shape3 = (samples, horizon_len, columns)
    mlp_value, mlp_back = jax.vjp(layer_norm, after_cross, gain_rows[2], shift_rows[2])
    mlp_in = mlp_value.astype(jnp.bfloat16)
    act_value, act_back = jax.vjp(jax.nn.gelu, hidden_pre)
    hidden = act_value.astype(jnp.bfloat16)
    grad_y3 = grad_out.astype(jnp.bfloat16)
    g_bdn = jnp.sum(grad_y3.astype(jnp.float32), axis=0)
    g_wdn = contract_rows(hidden, grad_y3)
    grad_pre = act_back(contract_cols(grad_y3, w_dn[layer_index]))[0].astype(jnp.bfloat16)
    g_bup = jnp.sum(grad_pre.astype(jnp.float32), axis=0)
    g_wup = contract_rows(mlp_in, grad_pre)
    grad_ln3 = mlp_back(contract_cols(grad_pre, w_up[layer_index]))
    grad_cross = grad_out + grad_ln3[0]
    cross_value, cross_back = jax.vjp(layer_norm, after_self, gain_rows[1], shift_rows[1])
    cross_in = cross_value.astype(jnp.bfloat16)
    grad_y2 = grad_cross.astype(jnp.bfloat16)
    g_cbo = jnp.sum(grad_y2.astype(jnp.float32), axis=0)
    g_wco = contract_rows(context_cross, grad_y2)
    grad_ctx2 = (
        contract_cols(grad_y2, w_co[layer_index])
        .astype(jnp.bfloat16)
        .reshape(shape3)
        .astype(jnp.float32)
    )
    query3 = cross_query.reshape(shape3)
    query_f = query3.astype(jnp.float32)
    score_list = cross_scores(query3, joined_keys, head_select, score_scale)
    joined_count = joined_keys.shape[1]
    probs_full = [jnp.exp(entry - log_cross) for entry in score_list]
    grad_probs = [
        head_sums(grad_ctx2 * joined_vals[:, index, None, :].astype(jnp.float32), head_select)
        for index in range(joined_count)
    ]
    inner = sum((probs_full[index] * grad_probs[index] for index in range(joined_count)))
    query_grad = jnp.zeros(shape3, jnp.float32)
    key_list = []
    val_list = []
    for index in range(joined_count):
        weight_low = head_expand(
            probs_full[index].astype(jnp.bfloat16).astype(jnp.float32), head_select
        )
        val_list.append(jnp.sum(weight_low * grad_ctx2, axis=1))
        score_grad = head_expand(
            (probs_full[index] * (grad_probs[index] - inner))
            .astype(jnp.bfloat16)
            .astype(jnp.float32),
            head_select,
        )
        query_grad = query_grad + score_grad * joined_keys[:, index, None, :].astype(jnp.float32)
        key_list.append(jnp.sum(score_grad * query_f, axis=1) * score_scale)
    grad_query = (query_grad * score_scale).reshape(tokens, columns).astype(jnp.bfloat16)
    grad_keys = jnp.stack(key_list, axis=1)
    grad_vals = jnp.stack(val_list, axis=1)
    time_grads = jnp.concatenate([grad_keys[:, 0], grad_vals[:, 0]], axis=1).astype(jnp.bfloat16)
    obs_key_grads = jnp.einsum(
        "so,snx->onx", select, grad_keys[:, 1:], precision=lax.Precision.HIGHEST
    ).reshape(-1, columns)
    obs_val_grads = jnp.einsum(
        "so,snx->onx", select, grad_vals[:, 1:], precision=lax.Precision.HIGHEST
    ).reshape(-1, columns)
    obs_grads = jnp.concatenate([obs_key_grads, obs_val_grads], axis=1).astype(jnp.bfloat16)
    g_wckv = contract_rows(memory, time_grads) + contract_rows(observed, obs_grads)
    g_cbv = jnp.sum(time_grads[:, columns:].astype(jnp.float32), axis=0) + jnp.sum(
        obs_grads[:, columns:].astype(jnp.float32), axis=0
    )
    grad_memory = contract_cols(time_grads, w_ckv[layer_index])
    g_cbq = jnp.sum(grad_query.astype(jnp.float32), axis=0)
    g_wcq = contract_rows(cross_in, grad_query)
    grad_ln2 = cross_back(contract_cols(grad_query, w_cq[layer_index]))
    grad_self = grad_cross + grad_ln2[0]
    self_value, self_back = jax.vjp(layer_norm, residual, gain_rows[0], shift_rows[0])
    normed = self_value.astype(jnp.bfloat16)
    grad_y1 = grad_self.astype(jnp.bfloat16)
    g_bso = jnp.sum(grad_y1.astype(jnp.float32), axis=0)
    g_wso = contract_rows(context_self, grad_y1)
    grad_ctx1 = contract_cols(grad_y1, w_so[layer_index]).astype(jnp.bfloat16).reshape(shape3)
    queries3 = queries.reshape(shape3)
    keys_wide = spread_heads(keys_self.reshape(shape3), head_select)
    vals_wide = spread_heads(vals_self.reshape(shape3), head_select)
    scores = self_scores(queries3, keys_wide, causal_wide, score_scale)
    probs_self = jnp.exp(scores - log_self)
    probs_self_low = probs_self.astype(jnp.bfloat16)
    vals_grad_wide = jnp.einsum(
        "sqj,sqd->sjd", probs_self_low, grad_ctx1, preferred_element_type=jnp.float32
    )
    grad_v1 = fold_heads(vals_grad_wide, head_select).reshape(tokens, columns).astype(jnp.bfloat16)
    grad_p1 = jnp.einsum("sqd,sjd->sqj", grad_ctx1, vals_wide, preferred_element_type=jnp.float32)
    inner_self = exact_product(
        (probs_self * grad_p1).reshape(-1, block_ones.shape[0]), block_ones
    ).reshape(scores.shape)
    grad_s1 = (probs_self * (grad_p1 - inner_self)).astype(jnp.bfloat16)
    grad_q1 = (
        (
            jnp.einsum("sqj,sjd->sqd", grad_s1, keys_wide, preferred_element_type=jnp.float32)
            * score_scale
        )
        .reshape(tokens, columns)
        .astype(jnp.bfloat16)
    )
    keys_grad_wide = jnp.einsum(
        "sqj,sqd->sjd", grad_s1, queries3, preferred_element_type=jnp.float32
    )
    grad_k1 = (
        (fold_heads(keys_grad_wide, head_select) * score_scale)
        .reshape(tokens, columns)
        .astype(jnp.bfloat16)
    )
    grad_qkv = jnp.concatenate([grad_q1, grad_k1, grad_v1], axis=1)
    g_win = contract_rows(normed, grad_qkv)
    g_bq = jnp.sum(grad_q1.astype(jnp.float32), axis=0)
    g_bv = jnp.sum(grad_v1.astype(jnp.float32), axis=0)
    grad_ln1 = self_back(contract_cols(grad_qkv, w_in[layer_index]))
    grad_in = grad_self + grad_ln1[0]
    gains_term = jnp.stack([grad_ln1[1], grad_ln2[1], grad_ln3[1]])
    shifts_term = jnp.stack(
        [grad_ln1[2], grad_ln2[2], grad_ln3[2], g_bq, g_bv, g_bso, g_cbq, g_cbv, g_cbo, g_bdn]
    )
    return (
        grad_in,
        (g_win, g_wso, g_wcq, g_wckv, g_wco, g_wup, g_wdn, gains_term, shifts_term, g_bup),
        grad_memory,
    )


def section_forward(section_input, weights, context):
    residual = section_input.astype(jnp.float32)
    residual, kept_values = layer_forward(residual, 0, weights, context)
    kept_all = [kept_values]
    return (residual.astype(jnp.bfloat16), tuple(kept_all))


def section_backward(grad_input, weights, context, kept_all):
    layer_total = weights[0].shape[0]
    gradient = grad_input.astype(jnp.float32)
    layer_terms = [None] * layer_total
    memory_grad = jnp.zeros(context[1].shape, jnp.float32)
    for layer_index in reversed(range(layer_total)):
        gradient, terms, grad_memory = layer_backward(
            gradient, layer_index, weights, context, kept_all[layer_index]
        )
        layer_terms[layer_index] = terms
        memory_grad = grad_memory
    stacked = tuple((jnp.stack([layer_terms[0][member]]) for member in range(10)))
    time_term = lax.dot_general(
        context[0].astype(jnp.float32),
        memory_grad,
        (((0,), (0,)), ((), ())),
        precision=lax.Precision.HIGHEST,
        preferred_element_type=jnp.float32,
    )
    return (gradient.astype(jnp.bfloat16), stacked + (time_term,))


def empty_slots(slot_count, leaf_value):
    return jnp.zeros((slot_count,) + leaf_value.shape, leaf_value.dtype)


def store_slot(slot_index, stacked, leaf_value):
    return lax.dynamic_update_index_in_dim(stacked, leaf_value, slot_index, 0)


def load_slot(slot_index, stacked):
    return lax.dynamic_index_in_dim(stacked, slot_index, 0, keepdims=False)


def add_where(flag_value, running, addend):
    return jnp.where(flag_value, running + addend, running)


def local(
    horizon,
    cotangent,
    obs_tokens,
    obs_repeat,
    noise_step,
    time_weight,
    self_in,
    self_out,
    cross_q,
    cross_kv,
    cross_out,
    mlp_up,
    mlp_down,
    gains,
    shifts,
    mlp_bias,
):
    sections = lax.axis_size("section")
    section_id = lax.axis_index("section")
    tick_count = sections + sections - 1
    slot_count = sections + 2
    columns = horizon.shape[-1]
    weights = (
        self_in,
        self_out,
        cross_q,
        cross_kv,
        cross_out,
        mlp_up,
        mlp_down,
        gains,
        shifts,
        mlp_bias,
    )
    obs_all = lax.all_gather(obs_tokens, "section", axis=0, tiled=True)

    def context_for(micro_index):
        return build_context(
            jnp.clip(micro_index, 0, sections - 1),
            noise_step,
            obs_repeat,
            obs_all,
            time_weight,
            columns,
        )

    inbound_queue = horizon[0]
    arriving = jnp.zeros_like(inbound_queue)
    kept_outputs = jnp.zeros((slot_count,) + inbound_queue.shape, jnp.bfloat16)
    kept_stash = None
    for tick_index in range(tick_count):
        micro_index = tick_index - section_id
        slot_index = jnp.clip(micro_index + 1, 0, slot_count - 1)
        section_input = jnp.where(section_id == 0, inbound_queue, arriving)
        section_output, kept_all = section_forward(section_input, weights, context_for(micro_index))
        kept_outputs = lax.dynamic_update_index_in_dim(kept_outputs, section_output, slot_index, 0)
        if kept_stash is None:
            kept_stash = jax.tree.map(partial(empty_slots, slot_count), kept_all)
        kept_stash = jax.tree.map(partial(store_slot, slot_index), kept_stash, kept_all)
        if tick_index + 1 < tick_count:
            arriving = passed_along(section_output, "section", 1)
        if tick_index + 1 < sections:
            inbound_queue = passed_along(inbound_queue, "section", -1)
    down_slot = cotangent[0]
    up_grad = jnp.zeros_like(down_slot)
    pred_slot = jnp.zeros_like(down_slot)
    zero_terms = tuple((jnp.zeros(weight.shape, jnp.float32) for weight in weights)) + (
        jnp.zeros((columns, columns), jnp.float32),
    )
    first_sum = zero_terms
    for tick_index in range(tick_count):
        order_index = tick_index - (sections - 1 - section_id)
        micro_index = sections - 1 - order_index
        is_valid = (order_index >= 0) & (order_index < sections)
        slot_index = jnp.clip(micro_index + 1, 0, slot_count - 1)
        grad_input = jnp.where(section_id == sections - 1, down_slot, up_grad)
        context = context_for(micro_index)
        kept_all = jax.tree.map(partial(load_slot, slot_index), kept_stash)
        grad_back, terms = section_backward(grad_input, weights, context, kept_all)
        first_sum = jax.tree.map(partial(add_where, is_valid), first_sum, terms)
        if tick_index >= sections - 1:
            pred_slot = jnp.where(
                section_id == sections - 1, kept_outputs[tick_index - sections + 2], pred_slot
            )
            down_slot = jnp.where(section_id == 0, grad_back, down_slot)
        if tick_index + 1 < tick_count:
            up_grad, pred_slot = passed_along((grad_back, pred_slot), "section", -1)
            down_slot = passed_along(down_slot, "section", 1)
    reduced = (
        lax.psum_scatter(first_sum[0], "dp", scatter_dimension=1, tiled=True),
        lax.psum_scatter(first_sum[1], "dp", scatter_dimension=1, tiled=True),
        lax.psum_scatter(first_sum[2], "dp", scatter_dimension=1, tiled=True),
        lax.psum_scatter(first_sum[3], "dp", scatter_dimension=1, tiled=True),
        lax.psum_scatter(first_sum[4], "dp", scatter_dimension=1, tiled=True),
        lax.psum_scatter(first_sum[5], "dp", scatter_dimension=1, tiled=True),
        lax.psum_scatter(first_sum[6], "dp", scatter_dimension=1, tiled=True),
        lax.psum_scatter(first_sum[7], "dp", scatter_dimension=2, tiled=True),
        lax.psum_scatter(first_sum[8], "dp", scatter_dimension=2, tiled=True),
        lax.psum_scatter(first_sum[9], "dp", scatter_dimension=1, tiled=True),
        lax.psum_scatter(first_sum[10], "dp", scatter_dimension=0, tiled=True),
    )
    time_grad = lax.psum(reduced[10], "section")
    return (
        pred_slot[None],
        down_slot[None],
        reduced[0],
        reduced[1],
        reduced[2],
        reduced[3],
        reduced[4],
        reduced[5],
        reduced[6],
        reduced[7],
        reduced[8],
        reduced[9],
        time_grad,
    )


def solution(mesh):
    return jax.shard_map(
        local,
        mesh=mesh,
        in_specs=(
            P("section", "dp", None),
            P("section", "dp", None),
            P("section", "dp", None, None),
            P(None, "dp", None),
            P(None, "dp"),
            P(),
            P("section", None, None),
            P("section", None, None),
            P("section", None, None),
            P("section", None, None),
            P("section", None, None),
            P("section", None, None),
            P("section", None, None),
            P("section", None, None),
            P("section", None, None),
            P("section", None),
        ),
        out_specs=(
            P("section", "dp", None),
            P("section", "dp", None),
            P("section", "dp", None),
            P("section", "dp", None),
            P("section", "dp", None),
            P("section", "dp", None),
            P("section", "dp", None),
            P("section", "dp", None),
            P("section", "dp", None),
            P("section", None, "dp"),
            P("section", None, "dp"),
            P("section", "dp"),
            P("dp", None),
        ),
        check_vma=False,
    )
```

profile of v0, /device:TPU:0, one launch (start us, length us, event | category | flops | bytes accessed | tf_op | source)
XLA Modules:
  0.0 2310.5 jit_solution(15887329352023029181)
XLA Ops:
  22.7 8.9 all_gather.3
  78.7 11.5 broadcast_in_dim.911
  397.3 4.8 collective-permute-start.16
  445.9 5.1 collective-permute-start.5
  523.2 4.8 collective-permute-start.6
  726.9 13.1 bitcast_multiply_fusion.13
  771.3 5.2 dynamic-slice_convert_fusion
  778.1 5.6 bitcast_dynamic-update-slice_fusion
  783.7 5.9 convert_reduce_fusion.6
  876.2 4.9 multiply_reduce_fusion.13
  886.9 4.5 dynamic-slice_reduce_fusion
  1007.7 4.9 fusion.288
  1014.4 6.1 convert_reduce_fusion.5
  1127.1 5.2 add_select_fusion.5
  1134.1 6.2 convert_reduce_fusion.4
  1240.7 6.0 convert_reduce_fusion.3
  1309.2 5.8 collective-permute-start.21
  1343.4 5.9 convert_reduce_fusion.2
  1445.1 6.2 convert_reduce_fusion.1
  1533.7 6.0 convert_reduce_fusion
  1656.8 4.9 fusion.378
  1679.5 39.8 %reduce-scatter.38.cloned.1.call-done = f32[128,1]{1,0:T(8,128)} async-done(((f32[1024,1]{1,0:T(8,128)}), f32[128,1]{1,0:T(8,128)}) %reduce-scatter.38.cloned.1.call-update) | async-done | bytes 528
  1720.7 62.2 %reduce-scatter.36.cloned.1.call-done = f32[32,10]{1,0:T(8,128)} async-done(((f32[256,10]{1,0:T(8,128)}), f32[32,10]{1,0:T(8,128)}) %reduce-scatter.36.cloned.1.call-update) | async-done | bytes 1296
  1784.5 62.3 %reduce-scatter.32.cloned.1.call-done = f32[32,256]{1,0:T(8,128)} async-done(((f32[256,256]{1,0:T(8,128)}), f32[32,256]{1,0:T(8,128)}) %reduce-scatter.32.cloned.1.call-update) | async-done | bytes 32784 | tf_op jit(solution)/shard_map/reduce_scatter | solution.py:520
  1846.8 11.4 psum.7
  1858.2 53.0 %reduce-scatter.20.cloned.1.call-done = f32[1,32,256]{2,1,0:T(8,128)} async-done(((f32[1,256,256]{2,1,0:T(8,128)}), f32[1,32,256]{2,1,0:T(8,128)}) %reduce-scatter.20.cloned.1.call-update) | async-done | bytes 32784 | tf_op jit(solution)/shard_map/reduce_scatter | solution.py:511
  1911.2 64.4 %reduce-scatter.22.cloned.1.call-done = f32[1,32,256]{2,1,0:T(8,128)} async-done(((f32[1,256,256]{2,1,0:T(8,128)}), f32[1,32,256]{2,1,0:T(8,128)}) %reduce-scatter.22.cloned.1.call-update) | async-done | bytes 32784 | tf_op jit(solution)/shard_map/reduce_scatter | solution.py:512
  1975.6 64.6 %reduce-scatter.26.cloned.1.call-done = f32[1,32,256]{2,1,0:T(8,128)} async-done(((f32[1,256,256]{2,1,0:T(8,128)}), f32[1,32,256]{2,1,0:T(8,128)}) %reduce-scatter.26.cloned.1.call-update) | async-done | bytes 32784 | tf_op jit(solution)/shard_map/reduce_scatter | solution.py:514
  2040.2 65.2 %reduce-scatter.24.cloned.1.call-done = f32[1,32,512]{2,1,0:T(8,128)} async-done(((f32[1,256,512]{2,1,0:T(8,128)}), f32[1,32,512]{2,1,0:T(8,128)}) %reduce-scatter.24.cloned.1.call-update) | async-done | bytes 65552 | tf_op jit(solution)/shard_map/reduce_scatter | solution.py:513
  2105.4 65.4 %reduce-scatter.18.cloned.1.call-done = f32[1,32,768]{2,1,0:T(8,128)} async-done(((f32[1,256,768]{2,1,0:T(8,128)}), f32[1,32,768]{2,1,0:T(8,128)}) %reduce-scatter.18.cloned.1.call-update) | async-done | bytes 98320 | tf_op jit(solution)/shard_map/reduce_scatter | solution.py:510
  2170.8 66.6 %reduce-scatter.28.cloned.1.call-done = f32[1,32,1024]{2,1,0:T(8,128)} async-done(((f32[1,256,1024]{2,1,0:T(8,128)}), f32[1,32,1024]{2,1,0:T(8,128)}) %reduce-scatter.28.cloned.1.call-update) | async-done | bytes 131088 | tf_op jit(solution)/shard_map/reduce_scatter | solution.py:515
  2237.4 66.4 %reduce-scatter.30.cloned.1.call-done = f32[1,128,256]{2,1,0:T(8,128)} async-done(((f32[1,1024,256]{2,1,0:T(8,128)}), f32[1,128,256]{2,1,0:T(8,128)}) %reduce-scatter.30.cloned.1.call-update) | async-done | bytes 131088 | tf_op jit(solution)/shard_map/reduce_scatter | solution.py:516
  (2785 shorter events, 1533.6 us)
Async XLA Ops:
  7.2 1670.8 %reduce-scatter.34.cloned.1.call-start = ((), (), s32[]{:S(2)}) async-start(), calls=%async_computation.19 | async-start | bytes 147456
  8.1 385.0 %collective-permute-start.9 = (bf16[1024,256]{0,1:T(8,128)(2,1)}, bf16[1024,256]{0,1:T(8,128)(2,1)}, u32[]{:S(2)}, u32[]{:S(2)}) collective-permute-start(bf16[1024,256]{0,1:T(8,128)(2,1)} %broadcast.1979), channel_id=1, source_target_pairs={{8,0},{16,8},{24,16},{9,1},{17,9},{25,17},{10,2},{18,10},{26,18},{... | collective-permute-start | bytes 1572872 | tf_op jit(solution)/shard_map/ppermute | solution.py:15
  11.5 316.4 %collective-permute-start = (bf16[1024,256]{0,1:T(8,128)(2,1)}, bf16[1024,256]{0,1:T(8,128)(2,1)}, u32[]{:S(2)}, u32[]{:S(2)}) collective-permute-start(bf16[1024,256]{0,1:T(8,128)(2,1)} %bitcast), channel_id=1, source_target_pairs={{8,0},{16,8},{24,16},{9,1},{17,9},{25,17},{10,2},{18,10},{26,18},{... | collective-permute-start | bytes 1572872 | tf_op jit(solution)/shard_map/ppermute | solution.py:15
  98.0 229.9 %collective-permute-start.1 = (bf16[1024,256]{0,1:T(8,128)(2,1)}, bf16[1024,256]{0,1:T(8,128)(2,1)}, u32[]{:S(2)}, u32[]{:S(2)}) collective-permute-start(bf16[1024,256]{0,1:T(8,128)(2,1)} %get-tuple-element.703), channel_id=1, source_target_pairs={{0,8},{8,16},{16,24},{1,9},{9,17},{17,25},{2,10},{10,18},{18,26},{... | collective-permute-start | bytes 1572872 | tf_op jit(solution)/shard_map/ppermute | solution.py:15
  103.2 294.1 %collective-permute-start.15 = (bf16[1024,256]{0,1:T(8,128)(2,1)}, bf16[1024,256]{0,1:T(8,128)(2,1)}, u32[]{:S(2)}, u32[]{:S(2)}) collective-permute-start(bf16[1024,256]{0,1:T(8,128)(2,1)} %bitcast.2673), channel_id=1, source_target_pairs={{0,8},{8,16},{16,24},{1,9},{9,17},{17,25},{2,10},{10,18},{18,26},{... | collective-permute-start | bytes 1572872 | tf_op jit(solution)/shard_map/ppermute | solution.py:15
  371.7 32.3 %collective-permute-start.3 = (bf16[1024,256]{0,1:T(8,128)(2,1)}, bf16[1024,256]{0,1:T(8,128)(2,1)}, u32[]{:S(2)}, u32[]{:S(2)}) collective-permute-start(bf16[1024,256]{0,1:T(8,128)(2,1)} %get-tuple-element.713), channel_id=1, source_target_pairs={{0,8},{8,16},{16,24},{1,9},{9,17},{17,25},{2,10},{10,18},{18,26},{... | collective-permute-start | bytes 1572872 | tf_op jit(solution)/shard_map/ppermute | solution.py:15
  393.1 77.3 %collective-permute-start.10 = (bf16[1024,256]{0,1:T(8,128)(2,1)}, bf16[1024,256]{0,1:T(8,128)(2,1)}, u32[]{:S(2)}, u32[]{:S(2)}) collective-permute-start(bf16[1024,256]{0,1:T(8,128)(2,1)} %collective-permute-done.9), channel_id=1, source_target_pairs={{8,0},{16,8},{24,16},{9,1},{17,9},{25,17},{10,2},{18,10},{26,18},{... | collective-permute-start | bytes 1572872 | tf_op jit(solution)/shard_map/ppermute | solution.py:15
  397.3 77.4 %collective-permute-start.16 = (bf16[1024,256]{0,1:T(8,128)(2,1)}, bf16[1024,256]{0,1:T(8,128)(2,1)}, u32[]{:S(2)}, u32[]{:S(2)}) collective-permute-start(bf16[1024,256]{0,1:T(8,128)(2,1)} %collective-permute-done.15), channel_id=1, source_target_pairs={{0,8},{8,16},{16,24},{1,9},{9,17},{17,25},{2,10},{10,18},{18,26},{... | collective-permute-start | bytes 1572872 | tf_op jit(solution)/shard_map/ppermute | solution.py:15
  445.9 35.0 %collective-permute-start.5 = (bf16[1024,256]{0,1:T(8,128)(2,1)}, bf16[1024,256]{0,1:T(8,128)(2,1)}, u32[]{:S(2)}, u32[]{:S(2)}) collective-permute-start(bf16[1024,256]{0,1:T(8,128)(2,1)} %get-tuple-element.723), channel_id=1, source_target_pairs={{0,8},{8,16},{16,24},{1,9},{9,17},{17,25},{2,10},{10,18},{18,26},{... | collective-permute-start | bytes 1572872 | tf_op jit(solution)/shard_map/ppermute | solution.py:15
  470.4 397.7 %collective-permute-start.11 = (bf16[1024,256]{0,1:T(8,128)(2,1)}, bf16[1024,256]{0,1:T(8,128)(2,1)}, u32[]{:S(2)}, u32[]{:S(2)}) collective-permute-start(bf16[1024,256]{0,1:T(8,128)(2,1)} %collective-permute-done.10), channel_id=1, source_target_pairs={{8,0},{16,8},{24,16},{9,1},{17,9},{25,17},{10,2},{18,10},{26,18},{... | collective-permute-start | bytes 1572872 | tf_op jit(solution)/shard_map/ppermute | solution.py:15
  474.7 764.2 %collective-permute-start.17 = (bf16[1024,256]{0,1:T(8,128)(2,1)}, bf16[1024,256]{0,1:T(8,128)(2,1)}, u32[]{:S(2)}, u32[]{:S(2)}) collective-permute-start(bf16[1024,256]{0,1:T(8,128)(2,1)} %collective-permute-done.16), channel_id=1, source_target_pairs={{0,8},{8,16},{16,24},{1,9},{9,17},{17,25},{2,10},{10,18},{18,26},{... | collective-permute-start | bytes 1572872 | tf_op jit(solution)/shard_map/ppermute | solution.py:15
  523.2 27.7 %collective-permute-start.6 = (bf16[1024,256]{0,1:T(8,128)(2,1)}, bf16[1024,256]{0,1:T(8,128)(2,1)}, u32[]{:S(2)}, u32[]{:S(2)}) collective-permute-start(bf16[1024,256]{0,1:T(8,128)(2,1)} %get-tuple-element.733), channel_id=1, source_target_pairs={{0,8},{8,16},{16,24},{1,9},{9,17},{17,25},{2,10},{10,18},{18,26},{... | collective-permute-start | bytes 1572872 | tf_op jit(solution)/shard_map/ppermute | solution.py:15
  592.8 26.1 %collective-permute-start.7 = (bf16[1024,256]{0,1:T(8,128)(2,1)}, bf16[1024,256]{0,1:T(8,128)(2,1)}, u32[]{:S(2)}, u32[]{:S(2)}) collective-permute-start(bf16[1024,256]{0,1:T(8,128)(2,1)} %get-tuple-element.743), channel_id=1, source_target_pairs={{0,8},{8,16},{16,24},{1,9},{9,17},{17,25},{2,10},{10,18},{18,26},{... | collective-permute-start | bytes 1572872 | tf_op jit(solution)/shard_map/ppermute | solution.py:15
  870.1 197.1 %collective-permute-start.12 = (bf16[1024,256]{0,1:T(8,128)(2,1)}, bf16[1024,256]{0,1:T(8,128)(2,1)}, u32[]{:S(2)}, u32[]{:S(2)}) collective-permute-start(bf16[1024,256]{0,1:T(8,128)(2,1)} %fusion.582), channel_id=1, source_target_pairs={{8,0},{16,8},{24,16},{9,1},{17,9},{25,17},{10,2},{18,10},{26,18},{... | collective-permute-start | bytes 1572872 | tf_op jit(solution)/shard_map/ppermute | solution.py:15
  903.0 109.6 %collective-permute-start.18 = (bf16[1024,256]{0,1:T(8,128)(2,1)}, bf16[1024,256]{0,1:T(8,128)(2,1)}, u32[]{:S(2)}, u32[]{:S(2)}) collective-permute-start(bf16[1024,256]{0,1:T(8,128)(2,1)} %add_convert_fusion.27), channel_id=1, source_target_pairs={{8,0},{16,8},{24,16},{9,1},{17,9},{25,17},{10,2},{18,10},{26,18},{... | collective-permute-start | bytes 1572872 | tf_op jit(solution)/shard_map/ppermute | solution.py:15
  1069.3 592.4 %collective-permute-start.13 = (bf16[1024,256]{0,1:T(8,128)(2,1)}, bf16[1024,256]{0,1:T(8,128)(2,1)}, u32[]{:S(2)}, u32[]{:S(2)}) collective-permute-start(bf16[1024,256]{0,1:T(8,128)(2,1)} %fusion.583), channel_id=1, source_target_pairs={{8,0},{16,8},{24,16},{9,1},{17,9},{25,17},{10,2},{18,10},{26,18},{... | collective-permute-start | bytes 1572872 | tf_op jit(solution)/shard_map/ppermute | solution.py:15
  1085.2 47.1 %collective-permute-start.19 = (bf16[1024,256]{0,1:T(8,128)(2,1)}, bf16[1024,256]{0,1:T(8,128)(2,1)}, u32[]{:S(2)}, u32[]{:S(2)}) collective-permute-start(bf16[1024,256]{0,1:T(8,128)(2,1)} %add_convert_fusion.26), channel_id=1, source_target_pairs={{8,0},{16,8},{24,16},{9,1},{17,9},{25,17},{10,2},{18,10},{26,18},{... | collective-permute-start | bytes 1572872 | tf_op jit(solution)/shard_map/ppermute | solution.py:15
  1201.4 37.4 %collective-permute-start.20 = (bf16[1024,256]{0,1:T(8,128)(2,1)}, bf16[1024,256]{0,1:T(8,128)(2,1)}, u32[]{:S(2)}, u32[]{:S(2)}) collective-permute-start(bf16[1024,256]{0,1:T(8,128)(2,1)} %add_convert_fusion.25), channel_id=1, source_target_pairs={{8,0},{16,8},{24,16},{9,1},{17,9},{25,17},{10,2},{18,10},{26,18},{... | collective-permute-start | bytes 1572872 | tf_op jit(solution)/shard_map/ppermute | solution.py:15
  1309.2 32.1 %collective-permute-start.21 = (bf16[1024,256]{0,1:T(8,128)(2,1)}, bf16[1024,256]{0,1:T(8,128)(2,1)S(1)}, u32[]{:S(2)}, u32[]{:S(2)}) collective-permute-start(bf16[1024,256]{0,1:T(8,128)(2,1)} %get-tuple-element.274), channel_id=1, source_target_pairs={{0,8},{8,16},{16,24},{1,9},{9,17},{17,25},{2,10},{10,18},{18,26},{... | collective-permute-start | bytes 1572872 | tf_op jit(solution)/shard_map/ppermute | solution.py:15
  1315.1 26.3 %collective-permute-start.22 = (bf16[1024,256]{0,1:T(8,128)(2,1)}, bf16[1024,256]{0,1:T(8,128)(2,1)}, u32[]{:S(2)}, u32[]{:S(2)}) collective-permute-start(bf16[1024,256]{0,1:T(8,128)(2,1)} %get-tuple-element.275), channel_id=1, source_target_pairs={{8,0},{16,8},{24,16},{9,1},{17,9},{25,17},{10,2},{18,10},{26,18},{... | collective-permute-start | bytes 1572872 | tf_op jit(solution)/shard_map/ppermute | solution.py:15
  1407.0 36.0 %collective-permute-start.23 = (bf16[1024,256]{0,1:T(8,128)(2,1)}, bf16[1024,256]{0,1:T(8,128)(2,1)S(1)}, u32[]{:S(2)}, u32[]{:S(2)}) collective-permute-start(bf16[1024,256]{0,1:T(8,128)(2,1)} %get-tuple-element.268), channel_id=1, source_target_pairs={{0,8},{8,16},{16,24},{1,9},{9,17},{17,25},{2,10},{10,18},{18,26},{... | collective-permute-start | bytes 1572872 | tf_op jit(solution)/shard_map/ppermute | solution.py:15
  1411.4 31.6 %collective-permute-start.24 = (bf16[1024,256]{0,1:T(8,128)(2,1)}, bf16[1024,256]{0,1:T(8,128)(2,1)}, u32[]{:S(2)}, u32[]{:S(2)}) collective-permute-start(bf16[1024,256]{0,1:T(8,128)(2,1)} %get-tuple-element.269), channel_id=1, source_target_pairs={{8,0},{16,8},{24,16},{9,1},{17,9},{25,17},{10,2},{18,10},{26,18},{... | collective-permute-start | bytes 1572872 | tf_op jit(solution)/shard_map/ppermute | solution.py:15
  1589.5 129.8 %reduce-scatter.38.cloned.1.call-start = ((), (), s32[]{:S(2)}) async-start(), calls=%async_computation.21 | async-start | bytes 589824
  1596.3 186.6 %reduce-scatter.36.cloned.1.call-start = ((), (), s32[]{:S(2)}) async-start(), calls=%async_computation.20 | async-start | bytes 147456
  1599.2 247.5 %reduce-scatter.32.cloned.1.call-start = ((), (), s32[]{:S(2)}) async-start(), calls=%async_computation.18 | async-start | bytes 294912 | tf_op jit(solution)/shard_map/reduce_scatter | solution.py:520
  1600.4 310.8 %reduce-scatter.20.cloned.1.call-start = ((), (), s32[]{:S(2)}) async-start(), calls=%async_computation.12 | async-start | bytes 294912 | tf_op jit(solution)/shard_map/reduce_scatter | solution.py:511
  1605.9 369.7 %reduce-scatter.22.cloned.1.call-start = ((), (), s32[]{:S(2)}) async-start(), calls=%async_computation.13 | async-start | bytes 294912 | tf_op jit(solution)/shard_map/reduce_scatter | solution.py:512
  1612.0 428.2 %reduce-scatter.26.cloned.1.call-start = ((), (), s32[]{:S(2)}) async-start(), calls=%async_computation.15 | async-start | bytes 294912 | tf_op jit(solution)/shard_map/reduce_scatter | solution.py:514
  1614.2 491.2 %reduce-scatter.24.cloned.1.call-start = ((), (), s32[]{:S(2)}) async-start(), calls=%async_computation.14 | async-start | bytes 589824 | tf_op jit(solution)/shard_map/reduce_scatter | solution.py:513
  1618.2 552.6 %reduce-scatter.18.cloned.1.call-start = ((), (), s32[]{:S(2)}) async-start(), calls=%async_computation.11 | async-start | bytes 884736 | tf_op jit(solution)/shard_map/reduce_scatter | solution.py:510
  1628.4 609.0 %reduce-scatter.28.cloned.1.call-start = ((), (), s32[]{:S(2)}) async-start(), calls=%async_computation.16 | async-start | bytes 1179648 | tf_op jit(solution)/shard_map/reduce_scatter | solution.py:515
  1641.1 662.7 %reduce-scatter.30.cloned.1.call-start = ((), (), s32[]{:S(2)}) async-start(), calls=%async_computation.17 | async-start | bytes 1179648 | tf_op jit(solution)/shard_map/reduce_scatter | solution.py:516
  (739 other events, 5677.7 us)
Sparse Core Ops, SparseCore 0:
  1589.6 65.3 reduce-scatter.33
  1658.3 60.8 reduce-scatter.37
  1722.9 59.9 reduce-scatter.35
  1786.5 60.2 reduce-scatter.31
  1850.9 60.2 reduce-scatter.19
  1915.3 60.2 reduce-scatter.21
  1979.8 60.2 reduce-scatter.25
  2044.5 60.8 reduce-scatter.23
  2109.3 61.4 reduce-scatter.17
  2175.0 62.3 reduce-scatter.27
  2241.4 62.3 reduce-scatter.29
where the time goes:
time: 2330 us; the launch traced here: 2310 us
  matrix products  655 us (28%)
  waiting for transfers between devices  615 us (26%)
  local copies, waits for them, and re-layouts  584 us (25%)
  other arithmetic  344 us (15%)
  starting transfers between devices  68.6 us (3%)
  between operations  24.3 us (1%)
    dot_general x140, matrix products, exact_product(): jnp.dot(left_side, right_side, precision=lax.Precision.HIGHEST, preferred...  249 us
    dot_general x56, matrix products, contract_rows(): lax.dot_general(left_side, right_side, (((0,), (0,)), ((), ())), preferre...  143 us
    unnamed x1563, local copies, waits for them, and re-layouts  118 us
    mul x63, local copies, waits for them, and re-layouts, cross_scores(): query_f * joined_keys[:, index, None, :].astype(jnp.float32)  117 us
    unnamed x14, waiting for transfers between devices  102 us
    dot_general x49, matrix products, contract_cols(): lax.dot_general(left_side, right_side, (((1,), (1,)), ((), ())), preferre...  100 us
    dot_general x71, matrix products, product(): return jnp.dot(left_side, right_side, preferred_element_type=jnp.float32)  89.9 us
    dynamic_update_slice x57, local copies, waits for them, and re-layouts, store_slot(): return lax.dynamic_update_index_in_dim(stacked, leaf_value, slot_index, 0)  77.3 us
  transfers between devices with their start and end apart: 38, of which 11 were waited for; matrix products, arithmetic and copies ran while one was open for 67% of the time, Pallas kernels for 0%

commit v1 on v0

v1 whole, which is shorter than its diff:
```python
import functools
import math

import jax
import jax.numpy as jnp
from jax import lax
from jax.experimental import pallas as pl
from jax.experimental.pallas import tpu as pltpu
from jax.sharding import PartitionSpec as P

HEADS = 4
VMEM_BYTES = 63 * 1024 * 1024
SUB = 128
F32 = jnp.float32
BF16 = jnp.bfloat16

W_IN, W_SO, W_CKV, W_CQ, W_CO, W_UP, W_END = 0, 768, 1024, 1536, 1792, 2048, 3072
SHIFT, BIAS, KEYSUM, VEC_ROWS = 3, 13, 17, 24
SENT = ((W_IN, 512), (512, W_CKV), (W_CKV, W_CQ), (W_CQ, W_UP), (W_UP, W_END))
DOWN_PIECE, PIECES = 5, 6
DOWN, UP, CROSS, SELF, TIME, VECTOR = range(6)
WIDTHS = (512, 512, 640, 384, 128, 128)
FORWARD_SELF, FORWARD_CROSS, FORWARD_FF = 1024, 1024, 1024
BACK_FF, BACK_CROSS, BACK_SELF = 1024, 1024, 1024
ROWS, NZ, NX = 32, 4, 2
GROUPS = NZ * NX
KEYS, WIDE = 24, 96


def dot(left, right):
    return jnp.dot(left, right, preferred_element_type=F32)


def dot_nt(left, right):
    return lax.dot_general(left, right, (((1,), (1,)), ((), ())), preferred_element_type=F32)


def dot_tn(left, right):
    return lax.dot_general(left, right, (((0,), (0,)), ((), ())), preferred_element_type=F32)


def iota(shape, axis):
    return lax.broadcasted_iota(jnp.int32, shape, axis)


def low(values):
    return jnp.asarray(values, BF16)


def normalize(values):
    center = values - jnp.mean(values, axis=-1, keepdims=True)
    scale = lax.rsqrt(jnp.mean(center * center, axis=-1, keepdims=True) + 1e-05)
    return center * scale, scale


def normalize_back(grad, unit, scale, gain):
    ahead = grad * unit
    grad_unit = grad * gain
    mean_grad = jnp.mean(grad_unit, axis=-1, keepdims=True)
    mean_along = jnp.mean(ahead * gain, axis=-1, keepdims=True)
    back = (grad_unit - mean_grad - unit * mean_along) * scale
    return back, jnp.sum(ahead, axis=0, keepdims=True), jnp.sum(grad, axis=0, keepdims=True)


def half_masks():
    lane = iota((1, SUB), 1)
    first = (lane < SUB // 2).astype(F32)
    return low(first), low(1.0 - first)


def add_low(left, right):
    return left + right


def place_row(column):
    size = column.shape[0]
    diagonal = iota((size, size), 0) == iota((size, size), 1)
    return jnp.sum(jnp.where(diagonal, column, 0.0), axis=0, keepdims=True)


def place_column(row):
    size = row.shape[1]
    diagonal = iota((size, size), 0) == iota((size, size), 1)
    return jnp.sum(jnp.where(diagonal, row, 0.0), axis=1, keepdims=True)


class Links:
    def __init__(self, w_s, wd_s, vec_s, wsend, wrecv, sets):
        self.w, self.wd, self.vec, self.wsend, self.wrecv, self.sets = w_s, wd_s, vec_s, wsend, wrecv, sets
        self.section = lax.axis_index("section")
        self.group = lax.axis_index("dp")
        self.core, self.y = self.section % 2, self.section // 2
        self.x, self.z = self.group % NX, self.group // NX
        self.x_peer = self.z * NX + (self.x + 1) % NX

    def relative(self, step):
        return (self.y + step // 2) % 2 * 2 + (self.core + step % 2) % 2

    def relation(self, block):
        return (self.y + block // 2) % 2 * 2 + (self.core + block % 2) % 2

    def z_peer(self, step):
        return (self.z + step) % NZ * NX + self.x

    def greet(self):
        barrier = pltpu.get_barrier_semaphore()
        peers = [{"section": self.relative(step)} for step in (1, 2, 3)]
        peers += [{"dp": self.x_peer}] + [{"dp": self.z_peer(step)} for step in range(1, NZ)]
        for peer in peers:
            pl.semaphore_signal(barrier, inc=1, device_id=peer, device_id_type=pl.DeviceIdType.MESH)
        pl.semaphore_wait(barrier, len(peers))

    def remote(self, src, dst, send, recv, peer):
        return pltpu.make_async_remote_copy(
            src_ref=src, dst_ref=dst, send_sem=send, recv_sem=recv, device_id=peer,
            device_id_type=pl.DeviceIdType.MESH,
        )

    def weight_copy(self, slot, block, piece, half, peer):
        array, lanes = (self.wd, slice(None)) if piece == DOWN_PIECE else (self.w, slice(*SENT[piece]))
        part = array.at[block, :, lanes]
        if half is not None:
            rows = array.shape[1] // 2
            part = array.at[block, pl.ds(pl.multiple_of(half * rows, rows), rows), lanes]
        return self.remote(part, part, self.wsend.at[slot], self.wrecv.at[slot], peer)

    def vector_copy(self, slot, block, peer):
        part = self.vec.at[block]
        return self.remote(part, part, self.wsend.at[slot], self.wrecv.at[slot], peer)

    def to_sibling(self, piece, block):
        return self.weight_copy(piece, block, piece, None, {"section": self.relative(1)})

    def over_y(self, piece, block):
        return self.weight_copy(PIECES + piece, block, piece, self.x, {"section": self.relative(2)})

    def over_x(self, piece, block, half):
        return self.weight_copy(2 * PIECES + piece, block, piece, half, {"dp": self.x_peer})

    def forwarded(self, piece, block, half, which):
        return self.weight_copy((3 + which) * PIECES + piece, block, piece, half, {"section": self.relative(1)})

    def vectors(self, step, block, peer):
        return self.vector_copy(5 * PIECES + step, block, {"section": peer})

    def start_y(self, when, pieces):
        @pl.when(when & (self.core == 1))
        def _():
            for piece in pieces:
                self.over_y(piece, self.section).start()

    def pass_first(self, piece, block):
        self.over_y(piece, block).wait_recv()
        self.over_x(piece, block, self.x).start()
        self.forwarded(piece, block, self.x, 0).start()

    def pass_second(self, piece, block):
        self.over_x(piece, block, 1 - self.x).wait_recv()
        self.forwarded(piece, block, 1 - self.x, 1).start()

    def pass_on(self, block, when, *works):
        @pl.when(self.relation(block) == 2 if when is True else when & (self.relation(block) == 2))
        def _():
            for stage, piece in works:
                if stage == 1 and piece == 0:
                    self.vectors(1, block, self.relative(2)).wait_recv()
                    self.vectors(2, block, self.relative(1)).start()
                (self.pass_first if stage == 1 else self.pass_second)(piece, block)

    def arrive(self, block, pieces):
        relation = self.relation(block)

        @pl.when(relation == 1)
        def _():
            if 0 in pieces:
                self.vectors(0, block, self.relative(1)).wait_recv()
            for piece in pieces:
                self.to_sibling(piece, block).wait_recv()

        @pl.when(relation == 3)
        def _():
            if 0 in pieces:
                self.vectors(2, block, self.relative(1)).wait_recv()
            for piece in pieces:
                self.forwarded(piece, block, self.x, 0).wait_recv()
                self.forwarded(piece, block, 1 - self.x, 1).wait_recv()

    def finish_weights(self):
        own, passed = self.section, self.relative(2)
        self.vectors(0, own, self.relative(1)).wait_send()
        self.vectors(1, own, self.relative(2)).wait_send()
        self.vectors(2, passed, self.relative(1)).wait_send()
        for piece in range(PIECES):
            self.to_sibling(piece, own).wait_send()
            self.over_y(piece, own).wait_send()
            self.over_x(piece, passed, self.x).wait_send()
            self.forwarded(piece, passed, self.x, 0).wait_send()
            self.forwarded(piece, passed, 1 - self.x, 1).wait_send()

    def near(self, kind):
        group_s, near_s, _, _, _, _, _, send, recv = self.sets[kind]
        return self.remote(group_s.at[1 - self.core], near_s, send.at[0], recv.at[0],
                           {"section": self.relative(1)})

    def row(self, kind):
        group_s, _, row_s, _, _, _, _, send, recv = self.sets[kind]
        return self.remote(group_s.at[self.core, :, 1 - self.x], row_s, send.at[1], recv.at[1],
                           {"dp": self.x_peer})

    def far(self, kind, step):
        far_s, _, _, fold_s, send, recv = self.sets[kind][3:]
        return self.remote(fold_s.at[(self.z + step) % NZ], far_s.at[step - 1],
                           send.at[1 + step], recv.at[1 + step], {"dp": self.z_peer(step)})

    def last(self, kind, step, peer):
        last_s, sum_s, _, send, recv = self.sets[kind][4:]
        slot = NZ + step
        return self.remote(sum_s, last_s.at[step - 1],
                           send.at[slot], recv.at[slot], {"section": peer})

    def after_near(self, kind):
        group_s, near_s = self.sets[kind][:2]
        self.near(kind).wait()
        group_s[self.core] = add_low(group_s[self.core], near_s[...])
        self.row(kind).start()

    def after_row(self, kind):
        group_s, row_s, fold_s = self.sets[kind][0], self.sets[kind][2], self.sets[kind][6]
        self.row(kind).wait()
        fold_s[...] = add_low(group_s[self.core, :, self.x], row_s[...])
        for step in range(1, NZ):
            self.far(kind, step).start()

    def sum_far(self, kind):
        far_s, _, sum_s, fold_s = self.sets[kind][3:7]
        for step in range(1, NZ):
            self.far(kind, step).wait()
        total = fold_s[self.z].astype(F32)
        for step in range(1, NZ):
            total = total + far_s[step - 1].astype(F32)
        sum_s[...] = low(total)

    def after_far(self, kind, block):
        self.sum_far(kind)
        relation = self.relation(block)

        @pl.when(relation > 0)
        def _():
            self.last(kind, relation, block).start()

    def halves(self, kind):
        last_s, sum_s = self.sets[kind][4:6]
        here = sum_s[...].astype(F32) + last_s[1].astype(F32)
        there = last_s[0].astype(F32) + last_s[2].astype(F32)
        return jnp.where(self.core == 0, here, there), jnp.where(self.core == 0, there, here)

    def after_last(self, kind, block, store):
        relation = self.relation(block)

        @pl.when(relation > 0)
        def _():
            self.last(kind, relation, block).wait_send()

        @pl.when(relation == 0)
        def _():
            for step in (1, 2, 3):
                self.last(kind, step, self.relative(step)).wait_recv()
            store(*self.halves(kind))

    def after_far_all(self, kind):
        self.sum_far(kind)
        for step in (1, 2, 3):
            self.last(kind, step, self.relative(step)).start()

    def after_last_all(self, kind):
        for step in (1, 2, 3):
            self.last(kind, step, self.relative(step)).wait()
        return self.halves(kind)


def block_kernel(remote, *refs):
    (x_ref, cot_ref, obs_ref, repeat_ref, noise_ref, tw_ref), refs = refs[:6], refs[6:]
    if remote:
        in_refs, refs = refs[:10], refs[10:]
        (pred_ref, grad_ref, in_out, so_out, cq_out, ckv_out, co_out, up_out, dn_out,
         gains_out, shifts_out, bias_out, time_out, hid_hbm, slope_hbm), refs = refs[:15], refs[15:]
    else:
        (w_hbm, wd_hbm, vec_hbm), refs = refs[:3], refs[3:]
        (pred_ref, grad_ref), dw_refs, refs = refs[:2], refs[2:6], refs[6:]
        (dvec_ref, time_out, hid_hbm, slope_hbm), refs = refs[:4], refs[4:]
    (unit_s, scale_s, qkv_s, prob_s, ctx_s, cq_s, cprob_s, cctx_s, hid_s, slope_s, dy_s, g_s,
     w_s, wd_s, vec_s, dvec_s, select_s, turned_s, tok_s, wide_s, folded_s, dmem_s, sinus_s, causal_s,
     own_s, flat_s, load_sem), groups, refs = refs[:27], refs[27:31], refs[31:]
    tokens, cols = x_ref.shape
    samples = noise_ref.shape[1]
    horizon = tokens // samples
    blocks = w_s.shape[0]
    per_sub = SUB // horizon
    score_scale = (cols // HEADS) ** (-0.5)
    section = lax.axis_index("section")
    ring = blocks - 1
    kept = ((hid_s, hid_hbm, load_sem.at[0]), (slope_s, slope_hbm, load_sem.at[1]))
    out_copies = [pltpu.make_async_copy(held.at[0], away, sem) for held, away, sem in kept]
    back_copies = [pltpu.make_async_copy(away, held.at[0], sem) for held, away, sem in kept]

    loads = [pltpu.make_async_copy(x_ref, pred_ref, load_sem.at[0]),
             pltpu.make_async_copy(cot_ref, grad_ref, load_sem.at[1])]
    if remote:
        gains_ref, shifts_ref, bias_ref = in_refs[7:]
        starts_at = (W_IN, W_SO, W_CKV, W_CQ, W_CO, W_UP)
        pieces = []
        for index, start in enumerate(starts_at):
            ref = in_refs[(0, 1, 3, 2, 4, 5)[index]]
            pieces.append(pltpu.make_async_copy(
                ref.at[0], w_s.at[section, :, start : start + ref.shape[2]], load_sem.at[2 + index]))
        pieces.append(pltpu.make_async_copy(in_refs[6].at[0], wd_s.at[section], load_sem.at[8]))
        for copy in pieces + loads:
            copy.start()
        vec_s[section] = jnp.zeros((VEC_ROWS, cols), F32)
        for row in range(SHIFT):
            vec_s[section, row : row + 1, :] = gains_ref[row]
        for row in range(SHIFT, BIAS):
            vec_s[section, row : row + 1, :] = shifts_ref[row - SHIFT]
        for part in range(4):
            vec_s[section, BIAS + part : BIAS + part + 1, :] = bias_ref[:, part * cols : (part + 1) * cols]
        sets = [(group,) + refs[2 + 8 * kind : 10 + 8 * kind] for kind, group in enumerate(groups)]
        sets += [refs[34 + 9 * index : 43 + 9 * index] for index in range(2)]
        links = Links(w_s, wd_s, vec_s, refs[0], refs[1], sets)
        links.greet()
        links.vectors(0, section, links.relative(1)).start()
        links.vectors(1, section, links.relative(2)).start()
        for piece, copies in enumerate((pieces[:1], pieces[1:2], pieces[2:3], pieces[3:5], pieces[5:6], pieces[6:])):
            for copy in copies:
                copy.wait()
            links.to_sibling(piece, section).start()

            @pl.when(links.core == 0)
            def _():
                links.over_y(piece, section).start()
    else:
        loads += [pltpu.make_async_copy(w_hbm, w_s, load_sem.at[2]),
                  pltpu.make_async_copy(wd_hbm, wd_s, load_sem.at[3]),
                  pltpu.make_async_copy(vec_hbm, vec_s, load_sem.at[4])]
        for copy in loads:
            copy.start()

    wide_masks = [jnp.concatenate([mask, mask], axis=1) for mask in half_masks()]
    lane_sub = iota((SUB, SUB), 1)
    row_sub = iota((SUB, SUB), 0)

    noise_row = noise_ref[pl.ds(section, 1), :].astype(F32)
    diagonal = iota((samples, samples), 0) == iota((samples, samples), 1)
    noise_col = jnp.sum(jnp.where(diagonal, noise_row, 0.0), axis=1, keepdims=True)
    half = cols // 2
    frequency = jnp.exp(iota((1, half), 1).astype(F32) * (-math.log(10000.0) / half))
    angles = noise_col * frequency
    sinus = low(jnp.concatenate([jnp.sin(angles), jnp.cos(angles)], axis=1))
    sinus_s[...] = sinus
    tok_s[:samples, :] = low(dot(sinus, tw_ref[...]))
    obs_count = repeat_ref.shape[-1]
    for index in range(obs_ref.shape[1]):
        tok_s[samples + index * obs_count : samples + (index + 1) * obs_count, :] = obs_ref[:, index, :]
    counts = low(repeat_ref[section].astype(F32))
    token_of = iota((obs_count, SUB), 1) - samples
    owner_of = iota((obs_count, SUB), 0)
    is_obs = token_of >= 0
    before = low((is_obs & (owner_of < token_of % obs_count)).astype(F32))
    upto = low((is_obs & (owner_of <= token_of % obs_count)).astype(F32))
    counts8 = jnp.broadcast_to(counts, (8, obs_count))
    starts = dot(counts8, before)[:1, :]
    ends = dot(counts8, upto)[:1, :]

    def select_rows(index, carried):
        key = iota((KEYS, SUB), 0) // per_sub
        lane = iota((KEYS, SUB), 1)
        sample = index * per_sub + iota((KEYS, SUB), 0) % per_sub
        sample_f = sample.astype(F32)
        time_hit = (key == 0) & (lane == sample)
        token = lane - samples
        owned = (sample_f >= starts) & (sample_f < ends)
        obs_hit = (token >= 0) & (token // obs_count == key - 1) & owned
        folded_s[index, :, :SUB] = (time_hit | obs_hit).astype(F32)
        return carried

    lax.fori_loop(0, tokens // SUB, select_rows, 0)
    selected = folded_s[...].reshape(-1, 2 * cols)[:, :SUB]
    select_s[...] = low(selected)
    selected = jnp.concatenate([selected, jnp.zeros((2 * SUB - selected.shape[0], SUB), F32)], axis=0)
    turned_s[...] = low(jnp.transpose(selected))
    same = row_sub // horizon == lane_sub // horizon
    causal_s[...] = jnp.where(same & (row_sub <= lane_sub), 0.0, -1e30)
    third = WIDE // 3
    own_s[...] = (iota((third, SUB), 0) % per_sub == iota((third, SUB), 1) // horizon).astype(F32)
    head_mask = (iota((third, cols), 0) // per_sub == iota((third, cols), 1) // (cols // HEADS)).astype(F32)
    dmem_s[...] = jnp.zeros_like(dmem_s)
    dvec_s[...] = jnp.zeros_like(dvec_s)
    for copy in loads:
        copy.wait()

    def vec(block, row):
        return vec_s[block, row : row + 1, :]

    def weight(block, start, stop):
        return w_s[block, :, start:stop]

    def condition(block):
        kv = dot(tok_s[...], weight(block, W_CKV, W_CQ))
        keys = low(kv[:, :cols])
        vals = low(kv[:, cols:] + vec(block, SHIFT + 7))

        spread = dot(select_s[...], jnp.concatenate([keys, vals], axis=1))
        both_masks = jnp.concatenate([head_mask, head_mask], axis=1)
        for index in range(tokens // SUB):
            for key in range(3):
                start = index * KEYS + key * per_sub
                copies = jnp.concatenate([spread[start : start + per_sub]] * HEADS, axis=0)
                wide_s[index, key * third : (key + 1) * third, :] = low(copies * both_masks)

    def fold(values):
        parts = []
        for part in thirds(values):
            part = part * head_mask
            parts.append(sum(part[head * per_sub : (head + 1) * per_sub] for head in range(HEADS)))
        return jnp.concatenate(parts, axis=0)

    def thirds(values):
        return [values[third * key : third * (key + 1)] for key in range(3)]

    def over_heads(values):
        return jnp.concatenate([values[:, :SUB], values[:, SUB:]], axis=0)

    def each_chunk(chunk, body):
        def at(step, carried):
            start = step * chunk
            body(pl.ds(start if isinstance(start, int) else pl.multiple_of(start, chunk), chunk), step)
            return carried

        if chunk == tokens:
            at(0, 0)
        else:
            lax.fori_loop(0, tokens // chunk, at, 0)

    def scale_of(block, rows, place):
        held = scale_s[rows, :]
        lane = iota(held.shape, 1)
        return jnp.sum(jnp.where(lane == 3 * block + place, held, 0.0), axis=1, keepdims=True)

    def keep_scale(block, rows, place, scale):
        held = scale_s[rows, :]
        scale_s[rows, :] = jnp.where(iota(held.shape, 1) == 3 * block + place, scale, held)

    def wide(values):
        return jnp.concatenate(values, axis=1)

    def both_heads(values):
        return jnp.concatenate([values * wide_masks[0], values * wide_masks[1]], axis=0)

    def both_pairs(values):
        zero = jnp.zeros((SUB, SUB), BF16)
        return jnp.concatenate([wide([values[:, :SUB], zero]), wide([zero, values[:, SUB:]])], axis=0)

    def forward(block, carried):
        after = jnp.minimum(block + 1, blocks - 1)
        if remote:
            links.arrive(block, (0, 1, 2))
            links.start_y(block == 0, range(3))
        condition(block)

        def self_attention(rows, step):
            x = pred_ref[rows, :].astype(F32)
            unit0, scale0 = normalize(x)
            unit_s[block, 0, rows, :] = low(unit0)
            a = low(unit0 * vec(block, 0) + vec(block, SHIFT))
            q = low((dot(a, weight(block, 0, cols)) + vec(block, SHIFT + 3)) * score_scale)
            k = low(dot(a, weight(block, cols, 2 * cols)))
            v = low(dot(a, weight(block, 2 * cols, 3 * cols)) + vec(block, SHIFT + 4))
            qkv_s[block, rows, :cols] = q
            qkv_s[block, rows, cols : 2 * cols] = k
            qkv_s[block, rows, 2 * cols :] = v
            causal2 = wide([causal_s[...]] * 2)
            parts = []
            for sub in range(rows.size // SUB):
                span = slice(sub * SUB, (sub + 1) * SUB)
                scores = dot_nt(both_pairs(k[span]), both_heads(q[span]))
                stacked = []
                for pair in range(2):
                    score = scores[pair * SUB : (pair + 1) * SUB] + causal2
                    top = jnp.max(score, axis=0, keepdims=True)
                    expo = jnp.exp(score - top)
                    prob = low(expo * (1.0 / jnp.sum(expo, axis=0, keepdims=True)))
                    prob_s[block, step * (rows.size // SUB) + sub, pair] = prob
                    stacked.append(over_heads(prob))
                both = dot_tn(wide(stacked), both_heads(v[span]))
                parts.append(low(wide([both[:SUB, :SUB], both[SUB:, SUB:]])))
            context = jnp.concatenate(parts, axis=0)
            ctx_s[block, rows, :] = context
            x = x + (dot(context, weight(block, W_SO, W_CKV)) + vec(block, SHIFT + 5))
            g_s[rows, :] = x
            keep_scale(block, rows, 0, scale0)
            if remote:
                links.pass_on(block, True, (1, 5), (2, 3), (2, 4))
                links.pass_on(after, block + 1 < blocks, (1, 0), (1, 1), (1, 2))
                links.start_y(block == 0, range(3, PIECES))


        each_chunk(FORWARD_SELF, self_attention)
        if remote:
            links.arrive(block, (3,))

        def cross_attention(rows, step):
            x = g_s[rows, :]
            unit1, scale1 = normalize(x)
            unit_s[block, 1, rows, :] = low(unit1)
            c = low(unit1 * vec(block, 1) + vec(block, SHIFT + 1))
            cq = low((dot(c, weight(block, W_CQ, W_CO)) + vec(block, SHIFT + 6)) * score_scale)
            cq_s[block, rows, :] = cq
            parts = []
            for sub in range(rows.size // SUB):
                index = step * (rows.size // SUB) + sub
                scores = thirds(dot_nt(wide_s[index, :, :cols], cq[sub * SUB : (sub + 1) * SUB]))
                top = jnp.maximum(jnp.maximum(scores[0], scores[1]), scores[2])
                expos = [jnp.exp(score - top) for score in scores]
                inverse = own_s[...] / (expos[0] + expos[1] + expos[2])
                prob = low(jnp.concatenate([expo * inverse for expo in expos], axis=0))
                cprob_s[block, index] = prob
                parts.append(low(dot_tn(prob, wide_s[index, :, cols:])))
            context = jnp.concatenate(parts, axis=0)
            cctx_s[block, rows, :] = context
            x = x + (dot(context, weight(block, W_CO, W_UP)) + vec(block, SHIFT + 8))
            unit2, scale2 = normalize(x)
            unit_s[block, 2, rows, :] = low(unit2)
            keep_scale(block, rows, 1, scale1)
            keep_scale(block, rows, 2, scale2)
            g_s[rows, :] = x + vec(block, SHIFT + 9)
            dy_s[0, rows, :] = low(unit2 * vec(block, 2) + vec(block, SHIFT + 2))
            if remote:
                links.pass_on(block, True, (2, 5))
                links.pass_on(after, block + 1 < blocks, (2, 0), (2, 1))

        each_chunk(FORWARD_CROSS, cross_attention)
        if remote:
            links.arrive(block, (4, 5))

        def feed_forward(rows, step):
            e = dy_s[0, rows, :]
            root = math.sqrt(2.0 / math.pi)
            cube = root * 0.044715
            for part in range(4):
                lanes = slice(part * cols, (part + 1) * cols)
                u = low(dot(e, weight(block, W_UP + part * cols, W_UP + (part + 1) * cols)) + vec(
                    block, BIAS + part
                ))
                square = u * u
                gate = jnp.tanh(u * (square * low(cube) + low(root))) * low(0.5) + low(0.5)
                hidden = u * gate
                slope = gate + hidden * (low(1.0) - gate) * (square * low(6.0 * cube) + low(2.0 * root))
                hid_s[block % ring, rows, lanes] = hidden
                slope_s[block % ring, rows, lanes] = slope
            pred_ref[rows, :] = low(g_s[rows, :] + dot(hid_s[block % ring, rows, :], wd_s[block]))
            if remote:
                links.pass_on(after, block + 1 < blocks, (2, 2), (1, 3), (1, 4))

        @pl.when(block == ring)
        def _():
            for copy in out_copies:
                copy.wait()

        each_chunk(FORWARD_FF, feed_forward)

        @pl.when(block == 0)
        def _():
            for copy in out_copies:
                copy.start()

        return carried

    if remote:
        links.pass_on(0, True, (1, 0), (1, 1), (2, 0), (1, 2), (2, 1), (1, 3), (2, 2), (1, 4))
    lax.fori_loop(0, blocks, forward, 0)

    def put(kind, start, value):
        width, taken = WIDTHS[kind], 0
        while taken < value.shape[1]:
            index, place = (start + taken) // width, (start + taken) % width
            count = min(value.shape[1] - taken, width - place)
            part = low(value[:, taken : taken + count]).reshape(NZ, NX, ROWS, count)
            groups[kind][index, :, :, :, place : place + count] = part
            taken += count

    def emit(block, kind):
        if remote:
            links.near(kind).start()
        else:
            copy = pltpu.make_async_copy(groups[kind], dw_refs[kind].at[block], load_sem.at[2])
            copy.start()
            copy.wait()

    def store_down(first, second):
        blocks_of = [value[:, q * SUB : (q + 1) * SUB] for value in (first, second) for q in range(4)]
        dn_out[...] = jnp.transpose(jnp.concatenate(blocks_of, axis=0))

    def store_up(first, second):
        up_out[...] = wide([first, second])

    def store_cross(first, second):
        joined = wide([first, second])
        ckv_out[...] = joined[:, : 2 * cols]
        for place, out in enumerate((cq_out, co_out, so_out)):
            out[...] = joined[:, (2 + place) * cols : (3 + place) * cols]

    def store_self(first, second):
        in_out[...] = wide([first, second])

    stores = (store_down, store_up, store_cross, store_self)

    def advance(works):
        if not remote:
            return
        for kind, stage, block, there in works:

            def run(kind=kind, stage=stage, block=block):
                if stage == 1:
                    links.after_near(kind)
                elif stage == 2:
                    links.after_row(kind)
                elif stage == 3:
                    links.after_far(kind, block)
                else:
                    links.after_last(kind, block, stores[kind])

            if there is True:
                run()
            else:
                pl.when(there)(run)

    def time_gradient():
        dmem = dmem_s[...]
        dmem_high = low(dmem)
        dmem_low = low(dmem - dmem_high.astype(F32))
        return dot_tn(sinus_s[...], dmem_high) + dot_tn(sinus_s[...], dmem_low)

    def emit_vectors():
        vectors = dvec_s[...].reshape(blocks * VEC_ROWS, cols)
        vectors = jnp.concatenate([vectors, jnp.zeros((SUB - blocks * VEC_ROWS, cols), F32)], axis=0)
        turned = jnp.transpose(vectors).reshape(GROUPS, ROWS, SUB)
        lane = iota((ROWS, SUB), 1) % VEC_ROWS
        rows_out = []
        for group in range(GROUPS):
            part, high = group // 2, group % 2
            piece = turned[group]
            for j in range(4):
                source = turned[4 * high + j]
                if j != part:
                    source = pltpu.roll(source, (j - part) % SUB, 1)
                piece = jnp.where(lane == BIAS + j, source, piece)
            rows_out.append(piece)
        turned = jnp.concatenate(rows_out, axis=0)
        for index in range(2):
            sets[VECTOR][0][index] = low(turned).reshape(NZ, NX, ROWS, SUB)
        links.near(VECTOR).start()

    def backward(turn, carried):
        block = blocks - 1 - turn
        earlier, before = block + 1, block + 2
        again, third_turn = turn > 0, turn > 1

        def add_vec(row, values):
            dvec_s[block, row : row + 1, :] += values

        def turn_over_ones(left):
            return jnp.concatenate([jnp.transpose(left), jnp.ones((16, tokens), BF16)], axis=0)

        def put_scaled(kind, start, unit_row, right, sum_rows):
            turned = turn_over_ones(unit_s[block, unit_row])
            gain = place_column(vec(block, unit_row))
            shift = place_column(vec(block, SHIFT + unit_row))
            parts = []
            for place, row in enumerate(sum_rows):
                both = dot(turned, right[:, place * cols : (place + 1) * cols])
                sums = both[cols : cols + 1]
                dvec_s[block, row : row + 1, :] = sums
                put(kind, start + place * cols, both[:cols] * gain + shift * sums)
                parts.append((both[:cols], sums))
            return parts

        def put_plain(kind, start, left, right, row):
            both = dot(turn_over_ones(left), right)
            dvec_s[block, row : row + 1, :] = both[cols : cols + 1]
            put(kind, start, both[:cols])

        @pl.when(block == 0)
        def _():
            for copy in back_copies:
                copy.wait()

        turned = jnp.transpose(grad_ref[...])
        for part in range(4):
            piece = low(dot(turned, hid_s[block % ring, :, part * cols : (part + 1) * cols]))
            for index in range(2):
                for x in range(NX):
                    for q in range(4):
                        row = SUB * index + ROWS * q
                        groups[DOWN][index, part, x, :, q * SUB : (q + 1) * SUB] = piece[
                            row : row + ROWS, x * SUB : (x + 1) * SUB
                        ]
        def feed_forward(rows, step):
            dy3 = grad_ref[rows, :]
            g = dy3.astype(F32)
            add_vec(SHIFT + 9, jnp.sum(g, axis=0, keepdims=True))
            for part in range(4):
                lanes = slice(part * cols, (part + 1) * cols)
                dh = dot_nt(dy3, wd_s[block, lanes, :])
                slope_s[block % ring, rows, lanes] = low(dh) * slope_s[block % ring, rows, lanes]
            de = dot_nt(slope_s[block % ring, rows, :], weight(block, W_UP, W_END))
            back, along, flat = normalize_back(
                de, unit_s[block, 2, rows, :].astype(F32), scale_of(block, rows, 2), vec(block, 2)
            )
            add_vec(2, along)
            add_vec(SHIFT + 2, flat)
            g = g + back
            g_s[rows, :] = g
            dy_s[0, rows, :] = low(g)

        each_chunk(BACK_FF, feed_forward)
        advance((
            (DOWN, 3, earlier, again), (CROSS, 2, earlier, again), (SELF, 1, earlier, again),
            (CROSS, 4, before, third_turn), (SELF, 4, before, third_turn),
        ))
        emit(block, DOWN)
        pl.when(turn == 0)(back_copies[0].start)

        put_scaled(UP, 0, 2, slope_s[block % ring], [BIAS + part for part in range(4)])
        condition(block)
        emit(block, UP)
        pl.when(turn == 0)(back_copies[1].start)

        def cross_attention(rows, step):
            dctx = low(dot_nt(dy_s[0, rows, :], weight(block, W_CO, W_UP)))
            for sub in range(rows.size // SUB):
                index = step * (rows.size // SUB) + sub
                span = pl.ds(index * SUB if isinstance(index, int) else pl.multiple_of(index * SUB, SUB), SUB)
                keys, vals = wide_s[index, :, :cols], wide_s[index, :, cols:]
                part = dctx[sub * SUB : (sub + 1) * SUB]
                prob = cprob_s[block, index]
                prob32 = prob.astype(F32)
                weighted = prob32 * dot_nt(vals, part)
                inner = sum(thirds(weighted))
                dscore = low(weighted - prob32 * jnp.concatenate([inner] * 3, axis=0))
                folded_s[index, :, :cols] = fold(dot(dscore, cq_s[block, span, :]))
                folded_s[index, :, cols:] = fold(dot(prob, part))
                cq_s[block, span, :] = low(dot_tn(dscore, keys) * score_scale)
            dcq = cq_s[block, rows, :]
            dc = dot_nt(dcq, weight(block, W_CQ, W_CO))
            back, along, flat = normalize_back(
                dc, unit_s[block, 1, rows, :].astype(F32), scale_of(block, rows, 1), vec(block, 1)
            )
            add_vec(1, along)
            add_vec(SHIFT + 1, flat)
            g = g_s[rows, :] + back
            g_s[rows, :] = g
            dy_s[1, rows, :] = low(g)

        each_chunk(BACK_CROSS, cross_attention)
        advance(((DOWN, 1, block, True), (DOWN, 4, earlier, again), (UP, 3, earlier, again)))

        folded = folded_s[...].reshape(-1, 2 * cols)
        dkv32 = dot(turned_s[:, : folded.shape[0]], low(folded))
        dkv = low(dkv32)
        add_vec(SHIFT + 7, jnp.sum(dkv32[:, cols:], axis=0, keepdims=True))
        dmem_s[...] += dot_nt(dkv[:samples], weight(block, W_CKV, W_CQ))
        put(CROSS, 0, dot_tn(tok_s[...], dkv))
        put_scaled(CROSS, 2 * cols, 1, cq_s[block], [SHIFT + 6])
        put_plain(CROSS, 3 * cols, cctx_s[block], dy_s[0], SHIFT + 8)
        put_plain(CROSS, 4 * cols, ctx_s[block], dy_s[1], SHIFT + 5)
        advance(((SELF, 2, earlier, again), (UP, 1, block, True)))
        emit(block, CROSS)
        if remote:

            @pl.when(block == 0)
            def _():
                dtime = time_gradient()
                for index in range(2):
                    part = low(dtime[:, index * SUB : (index + 1) * SUB])
                    sets[TIME][0][index] = part.reshape(NZ, NX, ROWS, SUB)
                links.near(TIME).start()

        def self_attention(rows, step):
            dctx = low(dot_nt(dy_s[1, rows, :], weight(block, W_SO, W_CKV)))
            for sub in range(rows.size // SUB):
                index = step * (rows.size // SUB) + sub
                span = pl.ds(index * SUB if isinstance(index, int) else pl.multiple_of(index * SUB, SUB), SUB)
                part = dctx[sub * SUB : (sub + 1) * SUB]
                queries, keys, values = (qkv_s[block, span, place * cols : (place + 1) * cols] for place in range(3))
                sides = (slice(0, SUB), slice(SUB, 2 * SUB))
                dstack = both_heads(part)
                qstack = both_heads(queries)
                kstack = both_heads(keys)
                probs = [prob_s[block, index, pair] for pair in range(2)]
                dprobs = dot_nt(both_pairs(values), dstack)
                dprobs = [dprobs[side] for side in sides]
                dscores = []
                for prob, dprob in zip(probs, dprobs):
                    prob32 = prob.astype(F32)
                    weighted = prob32 * dprob
                    dscores.append(low(weighted - prob32 * jnp.sum(weighted, axis=0, keepdims=True)))
                dq = dot_tn(wide([over_heads(dscore) for dscore in dscores]), kstack)
                dq = [dq[side, side] for side in sides]
                dk = dot(jnp.concatenate(dscores, axis=0), qstack)
                dk = [dk[side, side] for side in sides]
                dv = dot(jnp.concatenate(probs, axis=0), dstack)
                dv = [dv[side, side] for side in sides]
                qkv_s[block, span, :cols] = low(wide(dq) * score_scale)
                qkv_s[block, span, cols : 2 * cols] = low(wide(dk))
                qkv_s[block, span, 2 * cols :] = low(wide(dv))

        each_chunk(BACK_SELF, self_attention)
        advance((
            (CROSS, 3, earlier, again), (SELF, 3, earlier, again), (DOWN, 2, block, True),
            (CROSS, 1, block, True), (TIME, 1, block, block == 0), (UP, 4, earlier, again),
        ))

        gain_column, shift_column = 0.0, 0.0
        for place, (both, sums) in enumerate(
            put_scaled(SELF, 0, 0, qkv_s[block], (SHIFT + 3, KEYSUM, SHIFT + 4))
        ):
            matrix = weight(block, place * cols, (place + 1) * cols).astype(F32)
            gain_column += jnp.sum(both * matrix, axis=1, keepdims=True)
            shift_column += jnp.sum(sums * matrix, axis=1, keepdims=True)
        dvec_s[block, 0:1, :] = place_row(gain_column)
        dvec_s[block, SHIFT : SHIFT + 1, :] = place_row(shift_column)
        emit(block, SELF)
        if remote:
            pl.when(block == 0)(emit_vectors)

        def self_norm(rows, step):
            da = dot_nt(qkv_s[block, rows, :], weight(block, 0, 3 * cols))
            back, _, _ = normalize_back(
                da, unit_s[block, 0, rows, :].astype(F32), scale_of(block, rows, 0), vec(block, 0)
            )
            grad_ref[rows, :] = low(g_s[rows, :] + back)

        each_chunk(BACK_SELF, self_norm)
        advance(((UP, 2, block, True),))
        return carried

    lax.fori_loop(0, blocks, backward, 0)
    if not remote:
        time_out[...] = time_gradient()
        dvec_ref[...] = dvec_s[...]
        return

    links.after_last(CROSS, 1, store_cross)
    links.after_last(SELF, 1, store_self)
    links.after_near(SELF)
    links.after_near(VECTOR)
    links.after_far(DOWN, 0)
    links.after_row(CROSS)
    links.after_row(TIME)
    links.after_far(UP, 0)
    links.after_last(DOWN, 0, store_down)
    links.after_row(SELF)
    links.after_row(VECTOR)
    links.after_far(CROSS, 0)
    links.after_far_all(TIME)
    links.after_last(UP, 0, store_up)
    links.after_far(SELF, 0)
    links.after_far_all(VECTOR)
    links.after_last(CROSS, 0, store_cross)
    time_out[...] = wide(links.after_last_all(TIME))
    links.after_last(SELF, 0, store_self)
    mine, _ = links.after_last_all(VECTOR)
    padded = jnp.concatenate([mine, jnp.zeros((SUB - ROWS, SUB), F32)], axis=0)
    flat_s[...] = jnp.transpose(padded)
    mine = flat_s[pl.ds(pl.multiple_of(section * VEC_ROWS, 8), VEC_ROWS), :]
    for row in range(SHIFT):
        gains_out[row] = mine[row : row + 1, :ROWS]
    for row in range(SHIFT, BIAS):
        shifts_out[row - SHIFT] = mine[row : row + 1, :ROWS]
    bias = mine[BIAS : BIAS + 1, :]
    for part in range(1, 4):
        bias = bias + pltpu.roll(mine[BIAS + part : BIAS + part + 1, :], part * ROWS, 1)
    bias_out[...] = bias
    links.finish_weights()


def run_blocks(remote, x, cot, obs, repeat, noise, time_weight, *weights, interpret=False):
    tokens, cols = x.shape
    blocks = 4
    samples = noise.shape[1]
    vmem = pl.BlockSpec(memory_space=pltpu.VMEM)
    hbm = pl.BlockSpec(memory_space=pl.ANY)
    half_rows = (NZ, NX, ROWS)
    scratch = [
        pltpu.VMEM((blocks, 3, tokens, cols), BF16),
        pltpu.VMEM((tokens, SUB), F32),
        pltpu.VMEM((blocks, tokens, 3 * cols), BF16),
        pltpu.VMEM((blocks, tokens // SUB, 2, SUB, 2 * SUB), BF16),
        pltpu.VMEM((blocks, tokens, cols), BF16),
        pltpu.VMEM((blocks, tokens, cols), BF16),
        pltpu.VMEM((blocks, tokens // SUB, WIDE, SUB), BF16),
        pltpu.VMEM((blocks, tokens, cols), BF16),
        pltpu.VMEM((blocks - 1, tokens, 4 * cols), BF16),
        pltpu.VMEM((blocks - 1, tokens, 4 * cols), BF16),
        pltpu.VMEM((2, tokens, cols), BF16),
        pltpu.VMEM((tokens, cols), F32),
        pltpu.VMEM((blocks, cols, W_END), BF16),
        pltpu.VMEM((blocks, 4 * cols, cols), BF16),
        pltpu.VMEM((blocks, VEC_ROWS, cols), F32),
        pltpu.VMEM((blocks, VEC_ROWS, cols), F32),
        pltpu.VMEM((tokens // SUB * KEYS, SUB), BF16),
        pltpu.VMEM((SUB, 2 * SUB), BF16),
        pltpu.VMEM((SUB, cols), BF16),
        pltpu.VMEM((tokens // SUB, WIDE, 2 * cols), BF16),
        pltpu.VMEM((tokens // SUB, KEYS, 2 * cols), F32),
        pltpu.VMEM((samples, cols), F32),
        pltpu.VMEM((samples, cols), BF16),
        pltpu.VMEM((SUB, SUB), F32),
        pltpu.VMEM((WIDE // 3, SUB), F32),
        pltpu.VMEM((SUB, SUB), F32),
        pltpu.SemaphoreType.DMA((12,)),
    ]
    scratch += [pltpu.VMEM((2,) + half_rows + (width,), BF16) for width in WIDTHS[:TIME]]
    if remote:
        scratch += [pltpu.SemaphoreType.DMA((5 * PIECES + 3,))] * 2
        for kind, width in enumerate(WIDTHS):
            if kind >= TIME:
                scratch.append(pltpu.VMEM((2,) + half_rows + (width,), BF16))
            scratch += [
                pltpu.VMEM(half_rows + (width,), BF16),
                pltpu.VMEM((NZ, ROWS, width), BF16),
                pltpu.VMEM((NZ - 1, ROWS, width), BF16),
                pltpu.VMEM((3, ROWS, width), BF16),
                pltpu.VMEM((ROWS, width), BF16),
                pltpu.VMEM((NZ, ROWS, width), BF16),
                pltpu.SemaphoreType.DMA((4 + NZ,)),
                pltpu.SemaphoreType.DMA((4 + NZ,)),
            ]
        shapes = ((ROWS, 3 * cols), (ROWS, cols), (ROWS, cols), (ROWS, 2 * cols), (ROWS, cols),
                  (ROWS, 4 * cols), (4 * ROWS, cols), (SHIFT, 1, ROWS), (BIAS - SHIFT, 1, ROWS), (1, 4 * ROWS),
                  (ROWS, cols))
        outs = tuple(jax.ShapeDtypeStruct(shape, F32) for shape in shapes)
        in_specs = [hbm, hbm] + [vmem] * 4 + [hbm] * 7 + [vmem] * 3
        out_specs = (vmem,) * (2 + len(outs))
        params = pltpu.CompilerParams(
            vmem_limit_bytes=VMEM_BYTES, collective_id=0, has_side_effects=True)
    else:
        outs = (
            jax.ShapeDtypeStruct((blocks, VEC_ROWS, cols), F32),
            jax.ShapeDtypeStruct((cols, cols), F32),
        )
        outs = tuple(
            jax.ShapeDtypeStruct((blocks, 2) + half_rows + (width,), BF16) for width in WIDTHS[:TIME]
        ) + outs
        in_specs = [hbm, hbm] + [vmem] * 4 + [hbm] * 3
        out_specs = (vmem, vmem) + (hbm,) * 4 + (vmem, vmem)
        params = pltpu.CompilerParams(vmem_limit_bytes=VMEM_BYTES)
    low_out = jax.ShapeDtypeStruct((tokens, cols), BF16)
    away = jax.ShapeDtypeStruct((tokens, 4 * cols), BF16)
    return pl.pallas_call(
        functools.partial(block_kernel, remote),
        out_shape=(low_out, low_out) + outs + (away, away),
        in_specs=in_specs,
        out_specs=out_specs + (hbm, hbm),
        scratch_shapes=scratch,
        compiler_params=params,
        interpret=interpret,
    )(x, cot, obs, repeat, noise, time_weight, *weights)


def hand_out(*refs):
    count = (len(refs) - 1) // 3
    held, sem = refs[2 * count : 3 * count], refs[-1]
    arriving = [pltpu.make_async_copy(refs[i], held[i], sem.at[i]) for i in range(count)]
    leaving = []
    for copy in arriving:
        copy.start()
    for index in range(count):
        target = refs[count + index]
        if len(target.shape) > len(held[index].shape):
            target = target.at[0]
        arriving[index].wait()
        leaving.append(pltpu.make_async_copy(held[index], target, sem.at[index]))
        leaving[-1].start()
    for copy in leaving:
        copy.wait()


def finished(results):
    hbm = pl.BlockSpec(memory_space=pl.ANY)
    shapes = [(1,) + result.shape for result in results[:9]] + [result.shape for result in results[9:]]
    return pl.pallas_call(
        hand_out,
        out_shape=tuple(jax.ShapeDtypeStruct(shape, result.dtype) for shape, result in zip(shapes, results)),
        in_specs=[hbm] * len(results),
        out_specs=(hbm,) * len(results),
        scratch_shapes=[pltpu.VMEM(result.shape, result.dtype) for result in results]
        + [pltpu.SemaphoreType.DMA((len(results),))],
    )(*results)


def pack_weights(self_in, self_out, cross_q, cross_kv, cross_out, mlp_up, mlp_down):
    parts = (self_in, self_out, cross_kv, cross_q, cross_out, mlp_up)
    return jnp.concatenate([part[0] for part in parts], axis=1), mlp_down[0]


def pack_vectors(gains, shifts, mlp_bias):
    cols = gains.shape[-1]
    rows = jnp.concatenate([gains[0], shifts[0], mlp_bias.reshape(4, cols)], axis=0)
    return jnp.pad(rows, ((0, VEC_ROWS - rows.shape[0]), (0, 0)))


def natural(dweights):
    def joined(kind):
        parts = dweights[kind].reshape(-1, 2, GROUPS * ROWS, WIDTHS[kind])
        return jnp.concatenate([parts[:, 0], parts[:, 1]], axis=-1)

    blocks = dweights[DOWN].shape[0]
    down = dweights[DOWN].reshape(blocks, 2, GROUPS, ROWS, 4, SUB).transpose(0, 2, 5, 1, 4, 3)
    return joined(UP), joined(CROSS), joined(SELF), down.reshape(blocks, GROUPS * SUB, -1)


def gathered(data, packed_weights, packed_vectors):
    sections = lax.axis_size("section")
    groups = lax.axis_size("dp")
    cols = data[0].shape[-1]
    weights = [lax.all_gather(part, "section", axis=0) for part in packed_weights]
    vectors = lax.all_gather(packed_vectors, "section", axis=0)
    pred, grad, *dweights, dvectors, dtime, _, _ = run_blocks(False, *data, *weights, vectors)
    rows = cols // groups
    up, cross, own, down = natural(dweights)
    rest = jnp.concatenate([up, cross, own], axis=2).reshape(sections, groups, -1)
    down = down.reshape(sections, groups, -1)
    small = dvectors[:, :BIAS].reshape(sections, BIAS, groups, rows).transpose(0, 2, 1, 3)
    small = small.reshape(sections, groups, BIAS * rows)
    bias = dvectors[:, BIAS:KEYSUM].reshape(sections, groups, 4 * rows)
    term = jnp.broadcast_to(dtime.reshape(1, groups, rows * cols), (sections, groups, rows * cols))
    sent = jnp.concatenate([rest, down], axis=2).reshape(sections * groups, -1)
    sent_small = jnp.concatenate([small, bias, term], axis=2).reshape(sections * groups, -1)
    got = lax.psum_scatter(sent, ("section", "dp"), scatter_dimension=0, tiled=True)[0].astype(F32)
    got_small = lax.psum_scatter(sent_small, ("section", "dp"), scatter_dimension=0, tiled=True)[0]
    widths = (up.shape[-1], cross.shape[-1], own.shape[-1])
    split = sum(widths) * rows
    rest = got[:split].reshape(rows, sum(widths))
    down = got[split:].reshape(4 * rows, cols)
    small = got_small[: BIAS * rows].reshape(BIAS, rows)
    bias = got_small[BIAS * rows : (BIAS + 4) * rows].reshape(4, rows)
    term = got_small[(BIAS + 4) * rows :].reshape(rows, cols)
    up, cross, own = jnp.split(rest, (widths[0], widths[0] + widths[1]), axis=1)
    kv, query, out, self_out = jnp.split(cross, (2 * cols, 3 * cols, 4 * cols), axis=1)
    return (pred, grad, own, self_out, query, kv, out, up, down, small[:SHIFT], small[SHIFT:], bias, term)


def local(
    horizon, cotangent, obs_tokens, obs_repeat, noise_step, time_weight,
    self_in, self_out, cross_q, cross_kv, cross_out, mlp_up, mlp_down, gains, shifts, mlp_bias,
):
    cols = horizon.shape[-1]
    data = (horizon[0], cotangent[0], obs_tokens[0], obs_repeat, noise_step, time_weight)
    weights = (self_in, self_out, cross_q, cross_kv, cross_out, mlp_up, mlp_down)
    if lax.axis_size("dp") == GROUPS:
        vectors = (gains.transpose(1, 0, 2), shifts.transpose(1, 0, 2), mlp_bias)
        results = finished(run_blocks(True, *data, *weights, *vectors)[:-2])
        return results[:9] + (results[9].transpose(1, 0, 2), results[10].transpose(1, 0, 2)) + results[11:]
    results = gathered(data, pack_weights(*weights), pack_vectors(gains, shifts, mlp_bias))
    return tuple(result[None] for result in results[:11]) + (results[11].reshape(1, -1), results[12])


def solution(mesh):
    whole = P("section", None, None)
    return jax.shard_map(
        local,
        mesh=mesh,
        in_specs=(
            P("section", "dp", None), P("section", "dp", None), P("section", "dp", None, None),
            P(None, "dp", None), P(None, "dp"), P(),
            whole, whole, whole, whole, whole, whole, whole, whole, whole, P("section", None),
        ),
        out_specs=(P("section", "dp", None),) * 9
        + (P("section", None, "dp"), P("section", None, "dp"), P("section", "dp"), P("dp", None)),
        check_vma=False,
    )
```

time: 2330 us -> 139 us (0.06)
  matrix products: 655 us -> 0 us
  waiting for transfers between devices: 615 us -> 0 us
  local copies, waits for them, and re-layouts: 584 us -> 0 us
  other arithmetic: 344 us -> 0 us
  Pallas kernels: 0 us -> 138 us
  starting transfers between devices: 68.6 us -> 0 us
  between operations: 24.3 us -> 0.82 us
    dot_general x386 -> x0, matrix products: 655 us -> none  [the longest x140 249 us: exact_product(): jnp.dot(left_side, right_side, precision=lax.Precision.HIGHEST, preferred...]
    reduce_scatter x8 -> x0, waiting for transfers between devices: 508 us -> none  [the longest x1 66.6 us: local(): lax.psum_scatter(first_sum[5], 'dp', scatter_dimension=1, tiled=True)]
    reduce_sum x129 -> x0, other arithmetic: 170 us -> none  [the longest x21 55 us: layer_norm(): return center * lax.rsqrt(spread + 1e-05) * gain_row + shift_row]
    pallas_call x0 -> x2, Pallas kernels: none -> 138 us  [the longest x1 136 us: run_blocks(): pl.pallas_call(functools.partial(block_kernel, remote), out_shape=(low_ou...]
    unnamed x1563 -> x0, local copies, waits for them, and re-layouts: 118 us -> none
    mul x64 -> x0, local copies, waits for them, and re-layouts: 117 us -> none  [the longest x63 117 us: cross_scores(): query_f * joined_keys[:, index, None, :].astype(jnp.float32)]
    unnamed x14 -> x0, waiting for transfers between devices: 102 us -> none
    dynamic_update_slice x57 -> x0, local copies, waits for them, and re-layouts: 77.3 us -> none  [store_slot(): return lax.dynamic_update_index_in_dim(stacked, leaf_value, slot_index, 0)]
  transfers between devices with their start and end apart: 38 -> 0, of which waited for: 11 -> 0; matrix products, arithmetic and copies ran while one was open for 67% -> 0% of each run, Pallas kernels for 0% -> 0%
where the time goes in v1:
time: 139 us
  Pallas kernels  138 us (99%)
    pallas_call x1, Pallas kernels, run_blocks(): pl.pallas_call(functools.partial(block_kernel, remote), out_shape=(low_ou...  136 us

profile of v1, /device:TPU:0, one launch (start us, length us, event | category | flops | bytes accessed | tf_op | source)
XLA Modules:
  0.0 139.0 jit_solution(7222035324858211247)
XLA Ops:
  0.7 135.9 %shard_map.255 = (bf16[1024,256]{1,0:T(8,128)(2,1)}, bf16[1024,256]{1,0:T(8,128)(2,1)}, f32[32,768]{1,0:T(8,128)}, f32[32,256]{1,0:T(8,128)}, f32[32,256]{1,0:T(...) custom-call(bf16[1024,256]{1,0:T(8,128)(2,1)} %bitcast.7, ...), custom_call_target="tpu_custom_call" | custom-call | tf_op jit(solution)/shard_map/pallas_call | solution.py:959
  136.6 2.3 %shard_map.256 = (bf16[1,1024,256]{2,1,0:T(8,128)(2,1)}, bf16[1,1024,256]{2,1,0:T(8,128)(2,1)}, f32[1,32,768]{2,1,0:T(8,128)}, f32[1,32,256]{2,1,0:T(8,128)}, f3...) custom-call(bf16[1024,256]{1,0:T(8,128)(2,1)} %get-tuple-element.39., ...), custom_call_target="tpu_custom_call" | custom-call | tf_op jit(solution)/shard_map/pallas_call | solution.py:991

commit v2 on v1

--- a/solution.py
+++ b/solution.py
@@ -23,6 +23,7 @@
 FORWARD_SELF, FORWARD_CROSS, FORWARD_FF = 1024, 1024, 1024
 BACK_FF, BACK_CROSS, BACK_SELF = 1024, 1024, 1024
 ROWS, NZ, NX = 32, 4, 2
+TURNS = (UP, SELF)
 GROUPS = NZ * NX
 KEYS, WIDE = 24, 96
 
@@ -207,10 +208,15 @@
         return self.remote(group_s.at[self.core, :, 1 - self.x], row_s, send.at[1], recv.at[1],
                            {"dp": self.x_peer})
 
-    def far(self, kind, step):
+    def far_slot(self, kind, step, block):
+        return (block % 2) * (NZ - 1) + step - 1 if kind in TURNS else step - 1
+
+    def far(self, kind, step, block):
         far_s, _, _, fold_s, send, recv = self.sets[kind][3:]
-        return self.remote(fold_s.at[(self.z + step) % NZ], far_s.at[step - 1],
-                           send.at[1 + step], recv.at[1 + step], {"dp": self.z_peer(step)})
+        slot = self.far_slot(kind, step, block)
+        sem = slot + 2 if kind not in TURNS else 1 + step + (block % 2) * (NZ + 2)
+        return self.remote(fold_s.at[(self.z + step) % NZ], far_s.at[slot], send.at[sem], recv.at[sem],
+                           {"dp": self.z_peer(step)})
 
     def last(self, kind, step, peer):
         last_s, sum_s, _, send, recv = self.sets[kind][4:]
@@ -224,24 +230,24 @@
         group_s[self.core] = add_low(group_s[self.core], near_s[...])
         self.row(kind).start()
 
-    def after_row(self, kind):
+    def after_row(self, kind, block):
         group_s, row_s, fold_s = self.sets[kind][0], self.sets[kind][2], self.sets[kind][6]
         self.row(kind).wait()
         fold_s[...] = add_low(group_s[self.core, :, self.x], row_s[...])
         for step in range(1, NZ):
-            self.far(kind, step).start()
-
-    def sum_far(self, kind):
+            self.far(kind, step, block).start()
+
+    def sum_far(self, kind, block):
         far_s, _, sum_s, fold_s = self.sets[kind][3:7]
         for step in range(1, NZ):
-            self.far(kind, step).wait()
+            self.far(kind, step, block).wait()
         total = fold_s[self.z].astype(F32)
         for step in range(1, NZ):
-            total = total + far_s[step - 1].astype(F32)
+            total = total + far_s[self.far_slot(kind, step, block)].astype(F32)
         sum_s[...] = low(total)
 
     def after_far(self, kind, block):
-        self.sum_far(kind)
+        self.sum_far(kind, block)
         relation = self.relation(block)
 
         @pl.when(relation > 0)
@@ -268,7 +274,7 @@
             store(*self.halves(kind))
 
     def after_far_all(self, kind):
-        self.sum_far(kind)
+        self.sum_far(kind, 0)
         for step in (1, 2, 3):
             self.last(kind, step, self.relative(step)).start()
 
@@ -622,7 +628,7 @@
                 if stage == 1:
                     links.after_near(kind)
                 elif stage == 2:
-                    links.after_row(kind)
+                    links.after_row(kind, block)
                 elif stage == 3:
                     links.after_far(kind, block)
                 else:
@@ -723,14 +729,15 @@
 
         each_chunk(BACK_FF, feed_forward)
         advance((
-            (DOWN, 3, earlier, again), (CROSS, 2, earlier, again), (SELF, 1, earlier, again),
-            (CROSS, 4, before, third_turn), (SELF, 4, before, third_turn),
+            (DOWN, 3, earlier, again), (UP, 2, earlier, again), (SELF, 1, earlier, again),
+            (UP, 4, before, third_turn), (CROSS, 4, before, third_turn), (SELF, 4, before, third_turn),
         ))
         emit(block, DOWN)
         pl.when(turn == 0)(back_copies[0].start)
 
         put_scaled(UP, 0, 2, slope_s[block % ring], [BIAS + part for part in range(4)])
         condition(block)
+        advance(((CROSS, 2, earlier, again),))
         emit(block, UP)
         pl.when(turn == 0)(back_copies[1].start)
 
@@ -761,7 +768,7 @@
             dy_s[1, rows, :] = low(g)
 
         each_chunk(BACK_CROSS, cross_attention)
-        advance(((DOWN, 1, block, True), (DOWN, 4, earlier, again), (UP, 3, earlier, again)))
+        advance(((DOWN, 1, block, True), (DOWN, 4, earlier, again)))
 
         folded = folded_s[...].reshape(-1, 2 * cols)
         dkv32 = dot(turned_s[:, : folded.shape[0]], low(folded))
@@ -815,8 +822,8 @@
 
         each_chunk(BACK_SELF, self_attention)
         advance((
-            (CROSS, 3, earlier, again), (SELF, 3, earlier, again), (DOWN, 2, block, True),
-            (CROSS, 1, block, True), (TIME, 1, block, block == 0), (UP, 4, earlier, again),
+            (UP, 3, earlier, again), (CROSS, 3, earlier, again), (DOWN, 2, block, True),
+            (CROSS, 1, block, True), (TIME, 1, block, block == 0),
         ))
 
         gain_column, shift_column = 0.0, 0.0
@@ -840,7 +847,7 @@
             grad_ref[rows, :] = low(g_s[rows, :] + back)
 
         each_chunk(BACK_SELF, self_norm)
-        advance(((UP, 2, block, True),))
+        advance(((SELF, 3, earlier, again),))
         return carried
 
     lax.fori_loop(0, blocks, backward, 0)
@@ -849,17 +856,19 @@
         dvec_ref[...] = dvec_s[...]
         return
 
-    links.after_last(CROSS, 1, store_cross)
-    links.after_last(SELF, 1, store_self)
+    links.after_row(UP, 0)
     links.after_near(SELF)
     links.after_near(VECTOR)
     links.after_far(DOWN, 0)
-    links.after_row(CROSS)
-    links.after_row(TIME)
+    links.after_row(CROSS, 0)
+    links.after_row(TIME, 0)
+    links.after_last(UP, 1, store_up)
+    links.after_last(CROSS, 1, store_cross)
     links.after_far(UP, 0)
+    links.after_row(SELF, 0)
+    links.after_row(VECTOR, 0)
+    links.after_last(SELF, 1, store_self)
     links.after_last(DOWN, 0, store_down)
-    links.after_row(SELF)
-    links.after_row(VECTOR)
     links.after_far(CROSS, 0)
     links.after_far_all(TIME)
     links.after_last(UP, 0, store_up)
@@ -928,12 +937,12 @@
             scratch += [
                 pltpu.VMEM(half_rows + (width,), BF16),
                 pltpu.VMEM((NZ, ROWS, width), BF16),
-                pltpu.VMEM((NZ - 1, ROWS, width), BF16),
+                pltpu.VMEM(((2 if kind in TURNS else 1) * (NZ - 1), ROWS, width), BF16),
                 pltpu.VMEM((3, ROWS, width), BF16),
                 pltpu.VMEM((ROWS, width), BF16),
                 pltpu.VMEM((NZ, ROWS, width), BF16),
-                pltpu.SemaphoreType.DMA((4 + NZ,)),
-                pltpu.SemaphoreType.DMA((4 + NZ,)),
+                pltpu.SemaphoreType.DMA((3 + 2 * NZ,)),
+                pltpu.SemaphoreType.DMA((3 + 2 * NZ,)),
             ]
         shapes = ((ROWS, 3 * cols), (ROWS, cols), (ROWS, cols), (ROWS, 2 * cols), (ROWS, cols),
                   (ROWS, 4 * cols), (4 * ROWS, cols), (SHIFT, 1, ROWS), (BIAS - SHIFT, 1, ROWS), (1, 4 * ROWS),

time: 139 us -> 137 us (0.986)
  Pallas kernels: 138 us -> 136 us
    pallas_call x1, Pallas kernels: 136 us -> 134 us  [run_blocks(): pl.pallas_call(functools.partial(block_kernel, remote), out_shape=(low_ou...]
where the time goes in v2:
time: 137 us
  Pallas kernels  136 us (99%)
    pallas_call x1, Pallas kernels, run_blocks(): pl.pallas_call(functools.partial(block_kernel, remote), out_shape=(low_ou...  134 us

profile of v2, /device:TPU:0, one launch (start us, length us, event | category | flops | bytes accessed | tf_op | source)
XLA Modules:
  0.0 137.2 jit_solution(14967583427258571880)
XLA Ops:
  0.7 134.1 %shard_map.255 = (bf16[1024,256]{1,0:T(8,128)(2,1)}, bf16[1024,256]{1,0:T(8,128)(2,1)}, f32[32,768]{1,0:T(8,128)}, f32[32,256]{1,0:T(8,128)}, f32[32,256]{1,0:T(...) custom-call(bf16[1024,256]{1,0:T(8,128)(2,1)} %bitcast.7, ...), custom_call_target="tpu_custom_call" | custom-call | tf_op jit(solution)/shard_map/pallas_call | solution.py:968
  134.7 2.3 %shard_map.256 = (bf16[1,1024,256]{2,1,0:T(8,128)(2,1)}, bf16[1,1024,256]{2,1,0:T(8,128)(2,1)}, f32[1,32,768]{2,1,0:T(8,128)}, f32[1,32,256]{2,1,0:T(8,128)}, f3...) custom-call(bf16[1024,256]{1,0:T(8,128)(2,1)} %get-tuple-element.39., ...), custom_call_target="tpu_custom_call" | custom-call | tf_op jit(solution)/shard_map/pallas_call | solution.py:1000

commit v3 on v2

--- a/solution.py
+++ b/solution.py
@@ -469,7 +469,6 @@
         after = jnp.minimum(block + 1, blocks - 1)
         if remote:
             links.arrive(block, (0, 1, 2))
-            links.start_y(block == 0, range(3))
         condition(block)
 
         def self_attention(rows, step):
@@ -504,10 +503,10 @@
             g_s[rows, :] = x
             keep_scale(block, rows, 0, scale0)
             if remote:
-                links.pass_on(block, True, (1, 5), (2, 3), (2, 4))
+                links.pass_on(block, block > 0, (2, 3))
+                links.pass_on(block, block == 0, (2, 4), (2, 5))
                 links.pass_on(after, block + 1 < blocks, (1, 0), (1, 1), (1, 2))
-                links.start_y(block == 0, range(3, PIECES))
-
+                links.start_y(block == 0, range(PIECES))
 
         each_chunk(FORWARD_SELF, self_attention)
         if remote:
@@ -540,8 +539,8 @@
             g_s[rows, :] = x + vec(block, SHIFT + 9)
             dy_s[0, rows, :] = low(unit2 * vec(block, 2) + vec(block, SHIFT + 2))
             if remote:
-                links.pass_on(block, True, (2, 5))
-                links.pass_on(after, block + 1 < blocks, (2, 0), (2, 1))
+                links.pass_on(block, block > 0, (2, 4), (2, 5))
+                links.pass_on(after, block + 1 < blocks, (1, 3))
 
         each_chunk(FORWARD_CROSS, cross_attention)
         if remote:
@@ -564,7 +563,7 @@
                 slope_s[block % ring, rows, lanes] = slope
             pred_ref[rows, :] = low(g_s[rows, :] + dot(hid_s[block % ring, rows, :], wd_s[block]))
             if remote:
-                links.pass_on(after, block + 1 < blocks, (2, 2), (1, 3), (1, 4))
+                links.pass_on(after, block + 1 < blocks, (2, 0), (2, 1), (2, 2), (1, 4), (1, 5))
 
         @pl.when(block == ring)
         def _():
@@ -581,7 +580,7 @@
         return carried
 
     if remote:
-        links.pass_on(0, True, (1, 0), (1, 1), (2, 0), (1, 2), (2, 1), (1, 3), (2, 2), (1, 4))
+        links.pass_on(0, True, (1, 0), (1, 1), (2, 0), (1, 2), (2, 1), (1, 3), (2, 2), (1, 4), (2, 3), (1, 5))
     lax.fori_loop(0, blocks, forward, 0)
 
     def put(kind, start, value):

time: 137 us -> 136 us (level)
    pallas_call x1, Pallas kernels: 134 us -> 133 us  [run_blocks(): pl.pallas_call(functools.partial(block_kernel, remote), out_shape=(low_ou...]
where the time goes in v3:
time: 136 us
  Pallas kernels  135 us (99%)
    pallas_call x1, Pallas kernels, run_blocks(): pl.pallas_call(functools.partial(block_kernel, remote), out_shape=(low_ou...  133 us

profile of v3, /device:TPU:0, one launch (start us, length us, event | category | flops | bytes accessed | tf_op | source)
XLA Modules:
  0.0 135.8 jit_solution(15914431639046099573)
XLA Ops:
  0.7 132.7 %shard_map.255 = (bf16[1024,256]{1,0:T(8,128)(2,1)}, bf16[1024,256]{1,0:T(8,128)(2,1)}, f32[32,768]{1,0:T(8,128)}, f32[32,256]{1,0:T(8,128)}, f32[32,256]{1,0:T(...) custom-call(bf16[1024,256]{1,0:T(8,128)(2,1)} %bitcast.7, ...), custom_call_target="tpu_custom_call" | custom-call | tf_op jit(solution)/shard_map/pallas_call | solution.py:967
  133.3 2.3 %shard_map.256 = (bf16[1,1024,256]{2,1,0:T(8,128)(2,1)}, bf16[1,1024,256]{2,1,0:T(8,128)(2,1)}, f32[1,32,768]{2,1,0:T(8,128)}, f32[1,32,256]{2,1,0:T(8,128)}, f3...) custom-call(bf16[1024,256]{1,0:T(8,128)(2,1)} %get-tuple-element.39., ...), custom_call_target="tpu_custom_call" | custom-call | tf_op jit(solution)/shard_map/pallas_call | solution.py:999

commit v4 on v3

--- a/solution.py
+++ b/solution.py
@@ -285,20 +285,22 @@
 
 
 def block_kernel(remote, *refs):
-    (x_ref, cot_ref, obs_ref, repeat_ref, noise_ref, tw_ref), refs = refs[:6], refs[6:]
+    (x_ref, cot_ref), data_refs, refs = refs[:2], refs[2:6], refs[6:]
     if remote:
         in_refs, refs = refs[:10], refs[10:]
-        (pred_ref, grad_ref, in_out, so_out, cq_out, ckv_out, co_out, up_out, dn_out,
+        (pred_hbm, grad_hbm, in_out, so_out, cq_out, ckv_out, co_out, up_out, dn_out,
          gains_out, shifts_out, bias_out, time_out, hid_hbm, slope_hbm), refs = refs[:15], refs[15:]
     else:
         (w_hbm, wd_hbm, vec_hbm), refs = refs[:3], refs[3:]
-        (pred_ref, grad_ref), dw_refs, refs = refs[:2], refs[2:6], refs[6:]
+        (pred_hbm, grad_hbm), dw_refs, refs = refs[:2], refs[2:6], refs[6:]
         (dvec_ref, time_out, hid_hbm, slope_hbm), refs = refs[:4], refs[4:]
     (unit_s, scale_s, qkv_s, prob_s, ctx_s, cq_s, cprob_s, cctx_s, hid_s, slope_s, dy_s, g_s,
      w_s, wd_s, vec_s, dvec_s, select_s, turned_s, tok_s, wide_s, folded_s, dmem_s, sinus_s, causal_s,
-     own_s, flat_s, load_sem), groups, refs = refs[:27], refs[27:31], refs[31:]
+     own_s, flat_s, pred_ref, grad_ref, load_sem), groups, refs = refs[:29], refs[29:33], refs[33:]
+    small, refs = refs[:7], refs[7:]
+    obs_ref, repeat_ref, noise_ref, tw_ref, gains_ref, shifts_ref, bias_ref = small
     tokens, cols = x_ref.shape
-    samples = noise_ref.shape[1]
+    samples = sinus_s.shape[0]
     horizon = tokens // samples
     blocks = w_s.shape[0]
     per_sub = SUB // horizon
@@ -309,10 +311,16 @@
     out_copies = [pltpu.make_async_copy(held.at[0], away, sem) for held, away, sem in kept]
     back_copies = [pltpu.make_async_copy(away, held.at[0], sem) for held, away, sem in kept]
 
+    leaving = [pltpu.make_async_copy(pred_ref, pred_hbm, load_sem.at[20]),
+               pltpu.make_async_copy(grad_ref, grad_hbm, load_sem.at[21])]
+    sources = data_refs + (in_refs[7:] if remote else ())
+    fetched = [pltpu.make_async_copy(source, held, load_sem.at[12 + index])
+               for index, (source, held) in enumerate(zip(sources, small))]
+    for copy in fetched:
+        copy.start()
     loads = [pltpu.make_async_copy(x_ref, pred_ref, load_sem.at[0]),
              pltpu.make_async_copy(cot_ref, grad_ref, load_sem.at[1])]
     if remote:
-        gains_ref, shifts_ref, bias_ref = in_refs[7:]
         starts_at = (W_IN, W_SO, W_CKV, W_CQ, W_CO, W_UP)
         pieces = []
         for index, start in enumerate(starts_at):
@@ -322,6 +330,8 @@
         pieces.append(pltpu.make_async_copy(in_refs[6].at[0], wd_s.at[section], load_sem.at[8]))
         for copy in pieces + loads:
             copy.start()
+        for copy in fetched:
+            copy.wait()
         vec_s[section] = jnp.zeros((VEC_ROWS, cols), F32)
         for row in range(SHIFT):
             vec_s[section, row : row + 1, :] = gains_ref[row]
@@ -349,6 +359,8 @@
                   pltpu.make_async_copy(vec_hbm, vec_s, load_sem.at[4])]
         for copy in loads:
             copy.start()
+        for copy in fetched:
+            copy.wait()
 
     wide_masks = [jnp.concatenate([mask, mask], axis=1) for mask in half_masks()]
     lane_sub = iota((SUB, SUB), 1)
@@ -582,6 +594,7 @@
     if remote:
         links.pass_on(0, True, (1, 0), (1, 1), (2, 0), (1, 2), (2, 1), (1, 3), (2, 2), (1, 4), (2, 3), (1, 5))
     lax.fori_loop(0, blocks, forward, 0)
+    leaving[0].start()
 
     def put(kind, start, value):
         width, taken = WIDTHS[kind], 0
@@ -850,7 +863,10 @@
         return carried
 
     lax.fori_loop(0, blocks, backward, 0)
+    leaving[1].start()
     if not remote:
+        for copy in leaving:
+            copy.wait()
         time_out[...] = time_gradient()
         dvec_ref[...] = dvec_s[...]
         return
@@ -889,6 +905,8 @@
         bias = bias + pltpu.roll(mine[BIAS + part : BIAS + part + 1, :], part * ROWS, 1)
     bias_out[...] = bias
     links.finish_weights()
+    for copy in leaving:
+        copy.wait()
 
 
 def run_blocks(remote, x, cot, obs, repeat, noise, time_weight, *weights, interpret=False):
@@ -925,9 +943,15 @@
         pltpu.VMEM((SUB, SUB), F32),
         pltpu.VMEM((WIDE // 3, SUB), F32),
         pltpu.VMEM((SUB, SUB), F32),
-        pltpu.SemaphoreType.DMA((12,)),
+        pltpu.VMEM((tokens, cols), BF16),
+        pltpu.VMEM((tokens, cols), BF16),
+        pltpu.SemaphoreType.DMA((22,)),
     ]
     scratch += [pltpu.VMEM((2,) + half_rows + (width,), BF16) for width in WIDTHS[:TIME]]
+    parts = (obs, repeat, noise, time_weight) + tuple(weights[7:])
+    scratch += [pltpu.VMEM(part.shape, part.dtype) for part in parts]
+    if not remote:
+        scratch += [pltpu.VMEM((8, SUB), F32)] * 3
     if remote:
         scratch += [pltpu.SemaphoreType.DMA((5 * PIECES + 3,))] * 2
         for kind, width in enumerate(WIDTHS):
@@ -947,8 +971,8 @@
                   (ROWS, 4 * cols), (4 * ROWS, cols), (SHIFT, 1, ROWS), (BIAS - SHIFT, 1, ROWS), (1, 4 * ROWS),
                   (ROWS, cols))
         outs = tuple(jax.ShapeDtypeStruct(shape, F32) for shape in shapes)
-        in_specs = [hbm, hbm] + [vmem] * 4 + [hbm] * 7 + [vmem] * 3
-        out_specs = (vmem,) * (2 + len(outs))
+        in_specs = [hbm] * 16
+        out_specs = (hbm, hbm) + (vmem,) * len(outs)
         params = pltpu.CompilerParams(
             vmem_limit_bytes=VMEM_BYTES, collective_id=0, has_side_effects=True)
     else:
@@ -959,8 +983,8 @@
         outs = tuple(
             jax.ShapeDtypeStruct((blocks, 2) + half_rows + (width,), BF16) for width in WIDTHS[:TIME]
         ) + outs
-        in_specs = [hbm, hbm] + [vmem] * 4 + [hbm] * 3
-        out_specs = (vmem, vmem) + (hbm,) * 4 + (vmem, vmem)
+        in_specs = [hbm] * 9
+        out_specs = (hbm, hbm) + (hbm,) * 4 + (vmem, vmem)
         params = pltpu.CompilerParams(vmem_limit_bytes=VMEM_BYTES)
     low_out = jax.ShapeDtypeStruct((tokens, cols), BF16)
     away = jax.ShapeDtypeStruct((tokens, 4 * cols), BF16)

time: 136 us -> 136 us (level)
  no operation moved by 1% of the time
where the time goes in v4:
time: 136 us; the launch traced here: 135 us
  Pallas kernels  134 us (99%)
    pallas_call x1, Pallas kernels, run_blocks(): pl.pallas_call(functools.partial(block_kernel, remote), out_shape=(low_ou...  132 us

profile of v4, /device:TPU:0, one launch (start us, length us, event | category | flops | bytes accessed | tf_op | source)
XLA Modules:
  0.0 135.2 jit_solution(3880934668406713277)
XLA Ops:
  0.7 132.1 %shard_map.255 = (bf16[1024,256]{1,0:T(8,128)(2,1)}, bf16[1024,256]{1,0:T(8,128)(2,1)}, f32[32,768]{1,0:T(8,128)}, f32[32,256]{1,0:T(8,128)}, f32[32,256]{1,0:T(...) custom-call(bf16[1024,256]{1,0:T(8,128)(2,1)} %bitcast.7, ...), custom_call_target="tpu_custom_call" | custom-call | tf_op jit(solution)/shard_map/pallas_call | solution.py:991
  132.8 2.3 %shard_map.256 = (bf16[1,1024,256]{2,1,0:T(8,128)(2,1)}, bf16[1,1024,256]{2,1,0:T(8,128)(2,1)}, f32[1,32,768]{2,1,0:T(8,128)}, f32[1,32,256]{2,1,0:T(8,128)}, f3...) custom-call(bf16[1024,256]{1,0:T(8,128)(2,1)} %get-tuple-element.39., ...), custom_call_target="tpu_custom_call" | custom-call | tf_op jit(solution)/shard_map/pallas_call | solution.py:1023

commit v5 on v4

--- a/solution.py
+++ b/solution.py
@@ -343,16 +343,17 @@
         sets += [refs[34 + 9 * index : 43 + 9 * index] for index in range(2)]
         links = Links(w_s, wd_s, vec_s, refs[0], refs[1], sets)
         links.greet()
+        links.vectors(1, section, links.relative(2)).start()
         links.vectors(0, section, links.relative(1)).start()
-        links.vectors(1, section, links.relative(2)).start()
         for piece, copies in enumerate((pieces[:1], pieces[1:2], pieces[2:3], pieces[3:5], pieces[5:6], pieces[6:])):
             for copy in copies:
                 copy.wait()
-            links.to_sibling(piece, section).start()
 
             @pl.when(links.core == 0)
             def _():
                 links.over_y(piece, section).start()
+
+            links.to_sibling(piece, section).start()
     else:
         loads += [pltpu.make_async_copy(w_hbm, w_s, load_sem.at[2]),
                   pltpu.make_async_copy(wd_hbm, wd_s, load_sem.at[3]),

time: 136 us -> 136 us (level)
  no operation moved by 1% of the time
where the time goes in v5:
time: 136 us
  Pallas kernels  135 us (99%)
    pallas_call x1, Pallas kernels, run_blocks(): pl.pallas_call(functools.partial(block_kernel, remote), out_shape=(low_ou...  132 us

profile of v5, /device:TPU:0, one launch (start us, length us, event | category | flops | bytes accessed | tf_op | source)
XLA Modules:
  0.0 135.5 jit_solution(2043788274982638983)
XLA Ops:
  0.7 132.4 %shard_map.255 = (bf16[1024,256]{1,0:T(8,128)(2,1)}, bf16[1024,256]{1,0:T(8,128)(2,1)}, f32[32,768]{1,0:T(8,128)}, f32[32,256]{1,0:T(8,128)}, f32[32,256]{1,0:T(...) custom-call(bf16[1024,256]{1,0:T(8,128)(2,1)} %bitcast.7, ...), custom_call_target="tpu_custom_call" | custom-call | tf_op jit(solution)/shard_map/pallas_call | solution.py:992
  133.1 2.3 %shard_map.256 = (bf16[1,1024,256]{2,1,0:T(8,128)(2,1)}, bf16[1,1024,256]{2,1,0:T(8,128)(2,1)}, f32[1,32,768]{2,1,0:T(8,128)}, f32[1,32,256]{2,1,0:T(8,128)}, f3...) custom-call(bf16[1024,256]{1,0:T(8,128)(2,1)} %get-tuple-element.39., ...), custom_call_target="tpu_custom_call" | custom-call | tf_op jit(solution)/shard_map/pallas_call | solution.py:1024
